TPU v7x, 128 devices: a whole 4x4x4 slice. The times are simulated.
128 devices in a mesh: loop: 8 (over z_hi, y), chan: 16 (over x, z_lo, core).
Axes of the slice: x: 4, y: 4, z: 4 (z_hi: 2, z_lo: 2; z = z_hi * 2 + z_lo), core: 2. Of those that a mesh axis runs over, the one named last changes fastest.
Arguments:
- records: bfloat16 [256, 32768], P('loop', 'chan'), may hold values from -64 to 64
- dead_flags: int32 [256], P('loop'), may hold values 0 or 1
- starts: int32 [32], replicated, may hold values from 0 to 28672, as said below
- offsets: int32 [4], replicated, may hold values from 0 to 128, as said below
Outputs:
- cross_stack: float32 [256, 4, 4096], P(('loop', 'chan'))
Inputs may be any that keep to these rules, and one draw needn't show every extreme that they name: `starts`: rising; the first is 0 and the last 28672. `offsets`: the first is 0 and the last 128.
All inputs are finite; a program needn't handle non-finite values. No bound on the sum of `dead_flags` on one device may be relied on, other than what follows from the above.
Results may differ from a plain program's by a relative error of at most 0.0045.
Values may be sent and summed in bfloat16 or wider, within the bound.
No kernel may reach another device: no remote copies, remote signals or barrier semaphores. Data moves between devices by JAX's collectives and lax.ppermute only.
A program may use at most 192 MiB of HBM per device.

v0:
```python
import math

import jax
import jax.numpy as jnp
from jax import lax
from jax.sharding import PartitionSpec as P

NT = 32768
NF = 2048
NWIN = 32
RMW = 256
WB = 128
WIN = 4096


epsilon = 1e-06


def padded_2(block, sides, width):
    for axis, dim in sides:
        count = lax.axis_size(axis)
        forward = [(i, i + 1) for i in range(count - 1)]
        backward = [(target, source) for source, target in forward]
        low = lax.ppermute(
            lax.slice_in_dim(block, block.shape[dim] - width, None, axis=dim), axis, forward
        )
        high = lax.ppermute(lax.slice_in_dim(block, 0, width, axis=dim), axis, backward)
        block = jnp.concatenate([low, block, high], axis=dim)
    return block


def shifted(array, axis, by):
    size = lax.axis_size(axis)
    return lax.ppermute(array, axis, [(i, (i + by) % size) for i in range(size)])


def box_valid(padded, box_width):
    running = padded
    distance = 1
    while distance < box_width:
        running = running[..., :-distance] + running[..., distance:]
        distance *= 2
    return running[..., : padded.shape[-1] - box_width]


def box_sum(values, box_width):
    half_width = box_width // 2
    pad_spec = [(0, 0)] * (values.ndim - 1) + [(half_width, box_width - half_width)]
    return box_valid(jnp.pad(values, pad_spec), box_width)


def box_count(places, box_width, limit):
    upper = jnp.minimum(places + box_width // 2, limit)
    lower = jnp.maximum(places - box_width // 2, 0)
    return (upper - lower).astype(jnp.float32)


def normalize_shard(records, live_rows):
    length = records.shape[1]
    half_width = RMW // 2
    padded = padded_2(records, (("chan", 1),), half_width)
    values = padded.astype(jnp.float32) * live_rows[:, None]
    places = lax.axis_index("chan") * length + jnp.arange(length, dtype=jnp.int32)
    mean_level = box_valid(jnp.abs(values), 2 * half_width) / box_count(places, RMW, NT)[None, :]
    signal = values[:, half_width : half_width + length]
    return (signal / (mean_level + epsilon)).astype(jnp.bfloat16)


def cut_windows(normed, window_starts):

    def take_window(window_start):
        return lax.dynamic_slice_in_dim(normed, window_start, WIN, 1)

    return jax.vmap(take_window)(window_starts)


def spectra(segments):
    sample_index = jnp.arange(WIN, dtype=jnp.int32)[:, None]
    bin_width = min(NF, 256)
    real_parts = []
    imag_parts = []
    for first_bin in range(0, NF, bin_width):
        frequency = first_bin + jnp.arange(bin_width, dtype=jnp.int32)[None, :]
        phase_angle = (sample_index * frequency % WIN).astype(jnp.float32) * (2.0 * math.pi / WIN)
        table = jnp.concatenate([jnp.cos(phase_angle), -jnp.sin(phase_angle)], axis=1)
        table_high = table.astype(jnp.bfloat16)
        table_low = (table - table_high.astype(jnp.float32)).astype(jnp.bfloat16)
        product = jnp.dot(segments, table_high, preferred_element_type=jnp.float32)
        product = product + jnp.dot(segments, table_low, preferred_element_type=jnp.float32)
        real_parts.append(product[:, :bin_width])
        imag_parts.append(product[:, bin_width:])
    return (jnp.concatenate(real_parts, axis=1), jnp.concatenate(imag_parts, axis=1))


def whiten(real_part, imag_part):
    spectral_power = real_part * real_part + imag_part * imag_part
    bin_index = jnp.arange(NF, dtype=jnp.int32)
    smooth = box_sum(spectral_power, WB) / box_count(bin_index, WB, NF)[None, :]
    white_scale = 1.0 / jnp.sqrt(smooth + epsilon)
    white = jnp.concatenate([real_part * white_scale, imag_part * white_scale], axis=1).astype(
        jnp.bfloat16
    )
    return lax.optimization_barrier(white)


def add_pairs(running, own_panel, partner_panel, partner_row):
    panel_rows = partner_panel.shape[1]
    inside = (partner_row >= 0) & (partner_row < panel_rows)
    picked = jnp.take(partner_panel, jnp.clip(partner_row, 0, panel_rows - 1), axis=1)
    far_real = picked[..., :NF].astype(jnp.float32)
    far_imag = picked[..., NF:].astype(jnp.float32)
    own_real = own_panel[:, :, None, :NF].astype(jnp.float32)
    own_imag = own_panel[:, :, None, NF:].astype(jnp.float32)
    cross_real = jnp.sum(own_real * far_real + own_imag * far_imag, axis=0)
    cross_imag = jnp.sum(own_imag * far_real - own_real * far_imag, axis=0)
    cross_pair = jnp.concatenate([cross_real, cross_imag], axis=-1)
    return running + jnp.where(inside[:, :, None], cross_pair, 0.0)


def body(records, dead_flags, starts, offsets):
    block_rows = records.shape[0]
    live_block = (1 - dead_flags).astype(jnp.float32)
    outgoing = normalize_shard(records, live_block)
    owned_rows = lax.all_to_all(outgoing, "chan", split_axis=0, concat_axis=1, tiled=True)
    row_count = owned_rows.shape[0]
    segments = cut_windows(owned_rows, starts)
    real_part, imag_part = spectra(segments.reshape(-1, WIN))
    white = whiten(real_part, imag_part).reshape(NWIN, row_count, 2 * NF)
    own_panel = lax.all_to_all(white, "chan", split_axis=0, concat_axis=1, tiled=True)
    places = jnp.arange(block_rows, dtype=jnp.int32)[:, None] + offsets[None, :]
    running = jnp.zeros((block_rows, offsets.shape[0], 2 * NF), jnp.float32)
    running = add_pairs(running, own_panel, own_panel, places)
    shift_count = lax.axis_size("loop") // 2
    partner_panel = own_panel
    for distance in range(1, shift_count + 1):
        partner_panel = shifted(partner_panel, "loop", -1)
        running = add_pairs(running, own_panel, partner_panel, places - distance * block_rows)
    stacked = lax.psum_scatter(running, "chan", scatter_dimension=0, tiled=True)
    return stacked / NWIN


def solution(mesh):
    in_specs = (P("loop", "chan"), P("loop"), P(), P())
    out_specs = P(("loop", "chan"), None, None)
    return jax.shard_map(body, mesh=mesh, in_specs=in_specs, out_specs=out_specs, check_vma=False)
```

profile of v0, /device:TPU:1, one launch (start us, length us, event | category | flops | bytes accessed | tf_op | source)
XLA Modules:
  0.0 519.7 jit_solution(4578804214466256481)
XLA Ops:
  7.3 4.9 collective-permute-start
  12.2 1.9 collective-permute-start.1
  14.1 17.8 %sine_negate_fusion.7 = (f32[4096,256]{1,0:T(8,128)}, f32[4096,256]{1,0:T(8,128)}) fusion(), kind=kLoop, calls=%fused_computation.108 | loop fusion | flops 15728640 | bytes 8388608 | tf_op jit(solution)/shard_map/neg | solution.py:85
  32.2 18.0 %fusion.116 = (f32[4096,256]{1,0:T(8,128)}, f32[4096,256]{1,0:T(8,128)}) fusion(s32[256]{0:T(256)S(1)} %iota_add_fusion.9), kind=kLoop, calls=%fused_computation.193 | loop fusion | flops 15728640 | bytes 8389632 | tf_op jit(solution)/shard_map/cos | solution.py:85
  50.2 18.1 %fusion.115 = (f32[4096,256]{1,0:T(8,128)}, f32[4096,256]{1,0:T(8,128)}) fusion(s32[256]{0:T(256)S(1)} %iota_add_fusion.8), kind=kLoop, calls=%fused_computation.192 | loop fusion | flops 15728640 | bytes 8389632 | tf_op jit(solution)/shard_map/cos | solution.py:85
  68.3 18.1 %fusion.114 = (f32[4096,256]{1,0:T(8,128)}, f32[4096,256]{1,0:T(8,128)}) fusion(s32[256]{0:T(256)S(1)} %iota_add_fusion.7), kind=kLoop, calls=%fused_computation.191 | loop fusion | flops 15728640 | bytes 8389632 | tf_op jit(solution)/shard_map/cos | solution.py:85
  86.4 18.1 %fusion.113 = (f32[4096,256]{1,0:T(8,128)}, f32[4096,256]{1,0:T(8,128)}) fusion(s32[256]{0:T(256)S(1)} %iota_add_fusion.6), kind=kLoop, calls=%fused_computation.190 | loop fusion | flops 15728640 | bytes 8389632 | tf_op jit(solution)/shard_map/cos | solution.py:85
  104.5 18.0 %fusion.112 = (f32[4096,256]{1,0:T(8,128)}, f32[4096,256]{1,0:T(8,128)}) fusion(s32[256]{0:T(256)S(1)} %iota_add_fusion.5), kind=kLoop, calls=%fused_computation.189 | loop fusion | flops 15728640 | bytes 8389632 | tf_op jit(solution)/shard_map/cos | solution.py:85
  122.5 18.1 %fusion.111 = (f32[4096,256]{1,0:T(8,128)}, f32[4096,256]{1,0:T(8,128)}) fusion(s32[256]{0:T(256)S(1)} %iota_add_fusion.4), kind=kLoop, calls=%fused_computation.188 | loop fusion | flops 15728640 | bytes 8389632 | tf_op jit(solution)/shard_map/cos | solution.py:85
  140.6 18.0 %fusion.110 = (f32[4096,256]{1,0:T(8,128)}, f32[4096,256]{1,0:T(8,128)}) fusion(s32[256]{0:T(256)S(1)} %iota_add_fusion.3), kind=kLoop, calls=%fused_computation.187 | loop fusion | flops 15728640 | bytes 8389632 | tf_op jit(solution)/shard_map/cos | solution.py:85
  160.7 6.2 %all-to-all-start = ((bf16[16,2,2048]{2,1,0:T(2,128)(2,1)}), bf16[16,2,2048]{2,1,0:T(2,128)(2,1)S(1)}, u32[]{:S(2)}, u32[]{:S(2)}) async-start(bf16[16,2,2048]{2,1,0:T(2,128)(2,1)} %all_to_all.27), calls=%async_computation | async-start | bytes 262144 | tf_op jit(solution)/shard_map/all_to_all | solution.py:124
  167.1 5.8 %all-to-all-done = bf16[16,2,2048]{2,1,0:T(2,128)(2,1)S(1)} async-done(((bf16[16,2,2048]{2,1,0:T(2,128)(2,1)}), bf16[16,2,2048]{2,1,0:T(2,128)(2,1)S(1)}, u32[]{:S(2)}, u32[]{:S(2)}) %all-to-all-start) | async-done | bytes 131104 | tf_op jit(solution)/shard_map/all_to_all | solution.py:124
  172.9 43.2 %while.1 = (s32[]{:T(128)}, bf16[2,32768]{1,0:T(2,128)(2,1)S(1)}, s32[32,2]{0,1:T(2,128)S(1)}, bf16[32,2,4096]{2,1,0:T(2,128)(2,1)S(1)}, s32[]{:T(128)}) while((s32[]{:T(128)}, bf16[2,32768]{1,0:T(2,128)(2,1)S(1)}, s32[32,2]{0,1:T(2,128)S(1)}, bf16[32,2,4096]{2,1,0:T(2,128)(2,1)S(1)}, s32[]{:T(128)}) %tuple.70), condition=%wide.while_cond, body=%wide.while_body.sunk | while | flops 2 | bytes 32865 | solution.py:72
  216.4 4.4 fusion.8
  221.0 1.3 copy-done.1
  223.2 1.3 copy-done.14
  227.5 1.3 copy-done.12
  228.8 1.3 copy-done.13
  231.8 1.3 copy-done.10
  233.1 1.3 copy-done.11
  236.1 1.3 copy-done.8
  237.4 1.3 copy-done.9
  240.4 1.3 copy-done.6
  241.7 1.3 copy-done.7
  244.7 1.3 copy-done.4
  246.1 1.3 copy-done.5
  249.0 1.3 copy-done.2
  256.6 4.2 all-to-all-start.1
  262.7 7.8 %all-to-all-done.1 = bf16[32,2,4096]{2,1,0:T(2,128)(2,1)S(1)} async-done(((bf16[32,2,4096]{2,1,0:T(2,128)(2,1)}), bf16[32,2,4096]{2,1,0:T(2,128)(2,1)S(1)}, u32[]{:S(2)}, u32[]{:S(2)}) %all-to-all-start.1) | async-done | bytes 524320 | tf_op jit(solution)/shard_map/all_to_all | solution.py:129
  271.0 5.8 %collective-permute-start.2 = (bf16[2,32,4096]{2,0,1:T(2,128)(2,1)S(1)}, bf16[2,32,4096]{2,0,1:T(2,128)(2,1)S(1)}, u32[]{:S(2)}, u32[]{:S(2)}) collective-permute-start(bf16[2,32,4096]{2,0,1:T(2,128)(2,1)S(1)} %bitcast.48), channel_id=1, source_target_pairs={{0,112},{16,0},{32,16},{48,32},{64,48},{80,64},{96,80},{112,96},{1... | collective-permute-start | bytes 1572872 | tf_op jit(solution)/shard_map/ppermute | solution.py:34
  276.8 7.5 %gather_fusion = bf16[128,2,4096]{2,1,0:T(2,128)(2,1)S(1)} fusion(bf16[2,32,4096]{2,0,1:T(2,128)(2,1)S(1)} %bitcast.49, s32[1024]{0:T(1024)S(1)} %pad_clamp_fusion.4), kind=kCustom, calls=%fused_computation.clone | custom fusion | bytes 4194816 | tf_op jit(solution)/shard_map/jit(_take)/gather | solution.py:109
  284.3 3.4 fusion.100
  287.7 1.7 slice_convert_fusion.1
  289.4 3.2 collective-permute-start.3
  292.6 7.5 %gather_fusion.1 = bf16[128,2,4096]{2,1,0:T(2,128)(2,1)S(1)} fusion(bf16[2,32,4096]{2,0,1:T(2,128)(2,1)S(1)} %collective-permute-done.2, s32[1024]{0:T(1024)S(1)} %pad_clamp_fusion.3), kind=kCustom, calls=%fused_computation.1.clone | custom fusion | bytes 4194816 | tf_op jit(solution)/shard_map/jit(_take)/gather | solution.py:109
  300.1 3.5 fusion.101
  303.6 3.8 collective-permute-start.4
  307.4 7.5 %gather_fusion.2 = bf16[128,2,4096]{2,1,0:T(2,128)(2,1)S(1)} fusion(bf16[2,32,4096]{2,0,1:T(2,128)(2,1)S(1)} %collective-permute-done.3, s32[1024]{0:T(1024)S(1)} %pad_clamp_fusion.2), kind=kCustom, calls=%fused_computation.2.clone | custom fusion | bytes 4194816 | tf_op jit(solution)/shard_map/jit(_take)/gather | solution.py:109
  314.8 3.4 fusion.102
  318.2 3.0 collective-permute-start.5
  321.2 7.7 %gather_fusion.3 = bf16[128,2,4096]{2,1,0:T(2,128)(2,1)S(1)} fusion(bf16[2,32,4096]{2,0,1:T(2,128)(2,1)S(1)} %collective-permute-done.4, s32[1024]{0:T(1024)S(1)} %pad_clamp_fusion.1), kind=kCustom, calls=%fused_computation.3.clone | custom fusion | bytes 4194816 | tf_op jit(solution)/shard_map/jit(_take)/gather | solution.py:109
  328.9 3.4 fusion.103
  332.3 7.5 %gather_fusion.4 = bf16[128,2,4096]{2,1,0:T(2,128)(2,1)S(1)} fusion(bf16[2,32,4096]{2,0,1:T(2,128)(2,1)S(1)} %collective-permute-done.5, s32[1024]{0:T(1024)S(1)} %pad_clamp_fusion), kind=kCustom, calls=%fused_computation.4.clone | custom fusion | bytes 4194816 | tf_op jit(solution)/shard_map/jit(_take)/gather | solution.py:109
  339.8 2.1 fusion.104
  342.1 37.4 %fusion.97 = (f32[32,4,2048]{2,1,0:T(4,128)S(1)}, f32[32,4,2048]{2,1,0:T(4,128)S(1)}, f32[32,4,2048]{2,1,0:T(4,128)S(1)}, f32[32,4,2048]{2,1,0:T(4,128)S(1)}, f3...) fusion(f32[2,32,2048]{2,0,1:T(2,128)} %get-tuple-element.45, ...), kind=kLoop, calls=%fused_computation.169 | loop fusion | flops 23592960 | bytes 22020096 | tf_op jit(solution)/shard_map/reduce_sum | solution.py:114
  379.5 4.0 fusion.108
  384.8 126.0 %all-reduce.5.cloned.1.call-done = f32[32,4,4096]{2,1,0:T(4,128)} async-done(((f32[32,4,4096]{2,1,0:T(4,128)}), f32[32,4,4096]{2,1,0:T(4,128)}) %all-reduce.5.cloned.1.call-update) | async-done | bytes 2097168
  510.8 1.6 dynamic-slice_multiply_fusion
  (228 shorter events, 67.7 us)
Async XLA Ops:
  7.3 151.4 %collective-permute-start = (bf16[32,128]{1,0:T(8,128)(2,1)S(1)}, bf16[32,128]{1,0:T(8,128)(2,1)S(1)}, u32[]{:S(2)}, u32[]{:S(2)}) collective-permute-start(bf16[32,128]{1,0:T(8,128)(2,1)S(1)} %get-tuple-element.66), channel_id=1, source_target_pairs={{0,1},{1,2},{2,3},{3,4},{4,5},{5,6},{6,7},{7,8},{8,9},{9,10},{10,1... | collective-permute-start | bytes 24584 | tf_op jit(solution)/shard_map/ppermute | solution.py:24
  12.2 146.4 %collective-permute-start.1 = (bf16[32,128]{1,0:T(8,128)(2,1)S(1)}, bf16[32,128]{1,0:T(8,128)(2,1)S(1)}, u32[]{:S(2)}, u32[]{:S(2)}) collective-permute-start(bf16[32,128]{1,0:T(8,128)(2,1)S(1)} %get-tuple-element.67), channel_id=1, source_target_pairs={{1,0},{2,1},{3,2},{4,3},{5,4},{6,5},{7,6},{8,7},{9,8},{10,9},{11,1... | collective-permute-start | bytes 24584 | tf_op jit(solution)/shard_map/ppermute | solution.py:27
  14.1 17.9 %copy-start.20 = (s32[4]{0:T(128)S(1)}, s32[4]{0:T(128)}, u32[]{:S(2)}) copy-start(s32[4]{0:T(128)} %param.9) | copy-start | bytes 52
  14.1 18.0 %copy-start.21 = (s32[32]{0:T(128)S(1)}, s32[32]{0:T(128)}, u32[]{:S(2)}) copy-start(s32[32]{0:T(128)} %param.7) | copy-start | bytes 388
  140.6 18.0 %copy-start.19 = (bf16[32,2048]{1,0:T(8,128)(2,1)S(1)}, bf16[32,2048]{1,0:T(8,128)(2,1)}, u32[]{:S(2)}) copy-start(bf16[32,2048]{1,0:T(8,128)(2,1)} %param.6) | copy-start | bytes 393220
  158.8 8.1 %copy-start.22 = (s32[32]{0:T(128)S(1)}, s32[32]{0:T(128)}, u32[]{:S(2)}) copy-start(s32[32]{0:T(128)} %param.8) | copy-start | bytes 388
  160.7 12.2 %all-to-all-start = ((bf16[16,2,2048]{2,1,0:T(2,128)(2,1)}), bf16[16,2,2048]{2,1,0:T(2,128)(2,1)S(1)}, u32[]{:S(2)}, u32[]{:S(2)}) async-start(bf16[16,2,2048]{2,1,0:T(2,128)(2,1)} %all_to_all.27), calls=%async_computation | async-start | bytes 262144 | tf_op jit(solution)/shard_map/all_to_all | solution.py:124
  216.4 4.6 copy-start
  216.4 5.9 %copy-start.1 = (f32[4096,256]{1,0:T(8,128)S(1)}, f32[4096,256]{1,0:T(8,128)}, u32[]{:S(2)}) copy-start(f32[4096,256]{1,0:T(8,128)} %get-tuple-element.98) | copy-start | bytes 12582916
  222.3 2.2 copy-start.14
  222.3 3.5 copy-start.15
  226.6 2.2 copy-start.12
  226.6 3.5 copy-start.13
  230.9 2.2 copy-start.10
  230.9 3.5 copy-start.11
  235.2 2.2 copy-start.8
  235.2 3.5 copy-start.9
  239.5 2.2 copy-start.6
  239.6 3.5 copy-start.7
  243.9 2.2 copy-start.4
  243.9 3.5 copy-start.5
  248.2 2.2 copy-start.2
  248.2 3.5 copy-start.3
  256.6 13.8 %all-to-all-start.1 = ((bf16[32,2,4096]{2,1,0:T(2,128)(2,1)}), bf16[32,2,4096]{2,1,0:T(2,128)(2,1)S(1)}, u32[]{:S(2)}, u32[]{:S(2)}) async-start(bf16[32,2,4096]{2,1,0:T(2,128)(2,1)} %reshape.168), calls=%async_computation.1 | async-start | bytes 1048576 | tf_op jit(solution)/shard_map/all_to_all | solution.py:129
  260.7 250.1 %all-reduce.5.cloned.1.call-start = ((), (), s32[]{:S(2)}) async-start(), calls=%async_computation.2 | async-start | bytes 4194304
  271.0 18.4 %collective-permute-start.2 = (bf16[2,32,4096]{2,0,1:T(2,128)(2,1)S(1)}, bf16[2,32,4096]{2,0,1:T(2,128)(2,1)S(1)}, u32[]{:S(2)}, u32[]{:S(2)}) collective-permute-start(bf16[2,32,4096]{2,0,1:T(2,128)(2,1)S(1)} %bitcast.48), channel_id=1, source_target_pairs={{0,112},{16,0},{32,16},{48,32},{64,48},{80,64},{96,80},{112,96},{1... | collective-permute-start | bytes 1572872 | tf_op jit(solution)/shard_map/ppermute | solution.py:34
  289.4 14.2 %collective-permute-start.3 = (bf16[2,32,4096]{2,0,1:T(2,128)(2,1)S(1)}, bf16[2,32,4096]{2,0,1:T(2,128)(2,1)S(1)}, u32[]{:S(2)}, u32[]{:S(2)}) collective-permute-start(bf16[2,32,4096]{2,0,1:T(2,128)(2,1)S(1)} %collective-permute-done.2), channel_id=1, source_target_pairs={{0,112},{16,0},{32,16},{48,32},{64,48},{80,64},{96,80},{112,96},{1... | collective-permute-start | bytes 1572872 | tf_op jit(solution)/shard_map/ppermute | solution.py:34
  303.6 14.6 %collective-permute-start.4 = (bf16[2,32,4096]{2,0,1:T(2,128)(2,1)S(1)}, bf16[2,32,4096]{2,0,1:T(2,128)(2,1)S(1)}, u32[]{:S(2)}, u32[]{:S(2)}) collective-permute-start(bf16[2,32,4096]{2,0,1:T(2,128)(2,1)S(1)} %collective-permute-done.3), channel_id=1, source_target_pairs={{0,112},{16,0},{32,16},{48,32},{64,48},{80,64},{96,80},{112,96},{1... | collective-permute-start | bytes 1572872 | tf_op jit(solution)/shard_map/ppermute | solution.py:34
  318.2 14.1 %collective-permute-start.5 = (bf16[2,32,4096]{2,0,1:T(2,128)(2,1)S(1)}, bf16[2,32,4096]{2,0,1:T(2,128)(2,1)S(1)}, u32[]{:S(2)}, u32[]{:S(2)}) collective-permute-start(bf16[2,32,4096]{2,0,1:T(2,128)(2,1)S(1)} %collective-permute-done.4), channel_id=1, source_target_pairs={{0,112},{16,0},{32,16},{48,32},{64,48},{80,64},{96,80},{112,96},{1... | collective-permute-start | bytes 1572872 | tf_op jit(solution)/shard_map/ppermute | solution.py:34
  332.3 9.6 %copy-start.18 = (f32[2,32,2048]{2,0,1:T(2,128)S(1)}, f32[2,32,2048]{2,0,1:T(2,128)}, u32[]{:S(2)}) copy-start(f32[2,32,2048]{2,0,1:T(2,128)} %get-tuple-element.44) | copy-start | bytes 1572868
  339.8 2.1 copy-start.16
  339.8 2.2 copy-start.17
  379.5 4.1 copy-start.23
Sparse Core Ops, SparseCore 0:
  383.7 127.0 all-reduce.4
where the time goes:
time: 528 us; the launch traced here: 520 us
  other arithmetic  208 us (39%)
  waiting for transfers between devices  140 us (27%)
  local copies, waits for them, and re-layouts  107 us (20%)
  starting transfers between devices  33 us (6%)
  matrix products  17 us (3%)
  between operations  15.3 us (3%)
    cos x7, other arithmetic, spectra(): jnp.cos(phase_angle)  126 us
    unnamed x2, waiting for transfers between devices  126 us
    gather x96, local copies, waits for them, and re-layouts  42.8 us
    gather x5, local copies, waits for them, and re-layouts, add_pairs(): jnp.take(partner_panel, jnp.clip(partner_row, 0, panel_rows - 1), axis=1)  37.6 us
    reduce_sum x1, other arithmetic, add_pairs(): cross_real = jnp.sum(own_real * far_real + own_imag * far_imag, axis=0)  37.4 us
    unnamed x56, local copies, waits for them, and re-layouts  20.5 us
    neg x1, other arithmetic, spectra(): -jnp.sin(phase_angle)  17.8 us
    select_n x6, other arithmetic, add_pairs(): jnp.take(partner_panel, jnp.clip(partner_row, 0, panel_rows - 1), axis=1)  15.8 us
  transfers between devices with their start and end apart: 9, of which 3 were waited for; matrix products, arithmetic and copies ran while one was open for 37% of the time, Pallas kernels for 0%

commit v1 on v0

v1 whole, which is shorter than its diff:
```python
import functools
import math

import jax
import jax.numpy as jnp
import ml_dtypes
import numpy as np
from jax import lax
from jax.experimental import pallas as pl
from jax.experimental.pallas import tpu as pltpu
from jax.sharding import PartitionSpec as P

NT = 32768
NF = 2048
NWIN = 32
NOFF = 4
RMW = 256
WB = 128
WIN = 4096
LANES = 128
PHASES = 16
ROWS = 8
SEGS = ROWS * NWIN
GROUPS = NF // 256

epsilon = 1e-06


def split_table(table):
    high = table.astype(ml_dtypes.bfloat16)
    low = (table - high.astype(np.float64)).astype(ml_dtypes.bfloat16)
    return high, low


@functools.lru_cache(maxsize=None)
def tables():
    n2 = np.arange(256)[:, None]
    f2 = np.arange(LANES)[None, :]
    angle = 2.0 * math.pi * ((n2 * f2) % 256) / 256.0
    first = np.concatenate([np.cos(angle), -np.sin(angle)], axis=1)
    first_high, first_low = split_table(first)

    n1 = np.arange(PHASES)[:, None]
    angle = 2.0 * math.pi * ((n1 * f2) % WIN) / WIN
    twiddle = np.stack([np.cos(angle), np.sin(angle)], axis=1)
    twiddle = np.broadcast_to(twiddle[:, :, None, :], (PHASES, 2, ROWS, LANES))
    twiddle = np.ascontiguousarray(twiddle.reshape(2 * PHASES, ROWS, LANES)).astype(np.float32)

    sample = (np.arange(PHASES)[:, None] + PHASES * np.arange(256)[None, :])[:, :, None]
    group = np.arange(GROUPS)[None, None, :]
    angle = 2.0 * math.pi * (((1 + 2 * group) * sample) % 32) / 32.0
    middle = np.concatenate([np.cos(angle), np.sin(angle)], axis=2)
    high, low = split_table(middle)
    middle = np.zeros((PHASES, 256, LANES), ml_dtypes.bfloat16)
    middle[:, :, :16] = high
    middle[:, :, 16:32] = low

    lane = np.arange(LANES)
    upper = np.where(lane == 0, 128, 256 - lane)
    rows = np.concatenate([upper - 256, lane, upper, lane + 256])[:, None]
    columns = np.concatenate([lane, upper])[None, :]
    box = ((rows >= columns - WB // 2) & (rows < columns + WB // 2)).astype(ml_dtypes.bfloat16)

    bins = np.arange(GROUPS)[:, None] * 256 + np.concatenate([lane, upper])[None, :]
    count = np.minimum(bins + WB // 2, NF) - np.maximum(bins - WB // 2, 0)
    inverse = (1.0 / count).astype(np.float32).reshape(2 * GROUPS, 1, LANES)
    inverse = np.ascontiguousarray(np.broadcast_to(inverse, (2 * GROUPS, ROWS, LANES)))

    flip = np.zeros((LANES, LANES), np.float32)
    flip[(LANES - lane) % LANES, lane] = 1.0
    return first_high, first_low, twiddle, middle, box, inverse, flip


@functools.lru_cache(maxsize=None)
def deal_table():
    column = np.arange(256)
    table = np.zeros((256, 256), ml_dtypes.bfloat16)
    table[(column % 16) * 16 + column // 16, column] = 1.0
    return table


def lane_index(rows=ROWS):
    return lax.broadcasted_iota(jnp.int32, (rows, LANES), 1)


def roll_lanes(value, by):
    return pltpu.roll(value, by % LANES, 1)


def deal_kernel(records_ref, dead_ref, table_ref, out_ref, staged):
    rows = records_ref.shape[0]
    live = (1 - dead_ref[...]).astype(jnp.float32)
    lane = lane_index(rows)
    parts = [[None] * 8, [None] * 8]
    for chunk in range(8):
        product = jnp.dot(
            records_ref[:, chunk * 256 : (chunk + 1) * 256],
            table_ref[...],
            preferred_element_type=jnp.float32,
        )
        parts[0][chunk] = product[:, :LANES]
        parts[1][chunk] = product[:, LANES:]
    for half in range(2):
        current = parts[half]
        for bit in (1, 2, 4):
            step = 16 * bit
            keep = (lane // step) % 2 == 0
            following = list(current)
            for index in range(8):
                if index & bit == 0:
                    low, high = current[index], current[index | bit]
                    following[index] = jnp.where(keep, low, roll_lanes(high, step))
                    following[index | bit] = jnp.where(keep, roll_lanes(low, -step), high)
            current = following
        for index in range(8):
            staged[pl.ds(half * 8 + index, rows, stride=PHASES), :] = current[index] * live
    out_ref[...] = staged[...].reshape(rows, PHASES, LANES).astype(jnp.bfloat16)


def deal(records, dead_flags):
    rows = records.shape[0]
    vmem = pl.BlockSpec(memory_space=pltpu.VMEM)
    return pl.pallas_call(
        deal_kernel,
        out_shape=jax.ShapeDtypeStruct((rows, PHASES, LANES), jnp.bfloat16),
        in_specs=[vmem] * 3,
        out_specs=vmem,
        scratch_shapes=[pltpu.VMEM((rows * PHASES, LANES), jnp.float32)],
        compiler_params=pltpu.CompilerParams(vmem_limit_bytes=16 * 1024 * 1024),
    )(records, dead_flags.reshape(rows, 1), jnp.asarray(deal_table()))


def dft4(a, b, c, d):
    (ar, ai), (br, bi), (cr, ci), (dr, di) = a, b, c, d
    sr, si, tr, ti = ar + cr, ai + ci, ar - cr, ai - ci
    ur, ui, vr, vi = br + dr, bi + di, br - dr, bi - di
    return [(sr + ur, si + ui), (tr + vi, ti - vr), (sr - ur, si - ui), (tr - vi, ti + vr)]


def rotate(value, power):
    re, im = value
    power %= 16
    if power == 0:
        return value
    if power == 4:
        return (im, -re)
    root = math.sqrt(0.5)
    if power == 2:
        return ((re + im) * root, (im - re) * root)
    if power == 6:
        return ((im - re) * root, (re + im) * (-root))
    cos, sin = math.cos(2 * math.pi * power / 16), math.sin(2 * math.pi * power / 16)
    return (re * cos + im * sin, im * cos - re * sin)


def dft16(values):
    inner = [dft4(values[q], values[q + 4], values[q + 8], values[q + 12]) for q in range(4)]
    result = [None] * 16
    for k in range(4):
        outer = dft4(*[rotate(inner[q][k], q * k) for q in range(4)])
        for j in range(4):
            result[k + 4 * j] = outer[j]
    return result


def stack_kernel(
    starts_ref,
    parts_ref,
    high_ref,
    low_ref,
    twiddle_ref,
    middle_ref,
    box_ref,
    inverse_ref,
    flip_ref,
    out_ref,
    plain,
    before,
    after,
    normed,
    segments,
    middles,
    spectrum,
    power,
    smooth,
    folded,
):
    lane = lane_index()
    shards = parts_ref.shape[0]
    plain[...] = parts_ref[...].reshape(shards, ROWS * PHASES, LANES).astype(jnp.float32)

    totals = []
    for k in range(shards):
        level = [
            jnp.abs(plain[k, pl.ds(p, ROWS, stride=PHASES), :]) for p in range(PHASES)
        ]
        running = jnp.zeros((ROWS, LANES), jnp.float32)
        for p in range(PHASES):
            before[p, k] = running
            running = running + level[p]
        totals.append(running)
        running = jnp.zeros((ROWS, LANES), jnp.float32)
        for p in reversed(range(PHASES)):
            running = running + level[p]
            after[p, k] = running
    zero = jnp.zeros((ROWS, LANES), jnp.float32)

    def ahead(tiles, by):
        rolled = [roll_lanes(tile, -by) for tile in tiles] + [zero]
        return [jnp.where(lane < LANES - by, rolled[k], rolled[k + 1]) for k in range(len(tiles))]

    def behind(tiles, by):
        rolled = [zero] + [roll_lanes(tile, by) for tile in tiles]
        return [jnp.where(lane >= by, rolled[k + 1], rolled[k]) for k in range(len(tiles))]

    def plus(*lists):
        return [functools.reduce(lambda a, b: a + b, group) for group in zip(*lists)]

    two = plus(totals, ahead(totals, 1))
    four = plus(two, ahead(two, 2))
    columns = plus(ahead(four, 1), ahead(two, 5), ahead(totals, 7))
    past = totals
    for by in (1, 2, 4):
        past = plus(past, behind(past, by))
    columns = plus(columns, past)
    for k in range(shards):
        smooth[pl.ds(k * ROWS, ROWS), pl.ds(0, LANES)] = columns[k]

    def normalize(p, carry):
        first = behind([after[p, k] for k in range(shards)], 8)
        last = ahead([before[p, k] for k in range(shards)], 8)
        for k in range(shards):
            full = smooth[pl.ds(k * ROWS, ROWS), pl.ds(0, LANES)]
            total = full + first[k] + last[k]
            if k in (0, shards - 1):
                place = p + PHASES * (k * LANES + lane)
                count = jnp.minimum(place + RMW // 2, NT) - jnp.maximum(place - RMW // 2, 0)
                mean_level = total / count.astype(jnp.float32)
            else:
                mean_level = total * (1.0 / RMW)
            signal = plain[k, pl.ds(p, ROWS, stride=PHASES), :]
            ratio = signal / (mean_level + epsilon)
            normed[p, k] = ratio.astype(jnp.bfloat16).astype(jnp.float32)
        normed[p, shards] = zero
        return carry

    lax.fori_loop(0, PHASES, normalize, 0)

    def cut(w, carry):
        start = starts_ref[w]
        phase = start & (PHASES - 1)
        column = start >> 4
        for n1 in range(PHASES):
            place = phase + n1
            here = column + (place >> 4)
            tile = here >> 7
            by = here & (LANES - 1)
            p = place & (PHASES - 1)
            a, b, c = normed[p, tile], normed[p, tile + 1], normed[p, tile + 2]
            keep = lane >= by
            turn = (LANES - by) & (LANES - 1)
            segments[2 * n1, pl.ds(w, ROWS, stride=NWIN), :] = pltpu.roll(
                jnp.where(keep, a, b), turn, 1
            )
            segments[2 * n1 + 1, pl.ds(w, ROWS, stride=NWIN), :] = pltpu.roll(
                jnp.where(keep, b, c), turn, 1
            )
        return carry

    lax.fori_loop(0, NWIN, cut, 0)

    middles[...] = jnp.zeros_like(middles)

    def transform(n1, carry):
        left = jnp.concatenate([segments[2 * n1], segments[2 * n1 + 1]], axis=1)
        left = left.astype(jnp.bfloat16)
        product = jnp.dot(left, high_ref[...], preferred_element_type=jnp.float32)
        product = product + jnp.dot(left, low_ref[...], preferred_element_type=jnp.float32)
        middles[...] += jnp.dot(left, middle_ref[n1], preferred_element_type=jnp.float32)
        segments[2 * n1] = product[:, :LANES]
        segments[2 * n1 + 1] = product[:, LANES:]
        return carry

    lax.fori_loop(0, PHASES, transform, 0)

    zero_pair = jnp.zeros((SEGS, LANES), jnp.bfloat16)
    power[:, pl.ds(0, LANES)] = zero_pair
    power[:, pl.ds((2 * GROUPS + 1) * LANES, LANES)] = zero_pair

    def combine(pair, carry):
        powers = []
        for part in range(2):
            rows = pl.ds(pl.multiple_of(pair * 16 + part * ROWS, ROWS), ROWS)
            values = []
            for n1 in range(PHASES):
                re, im = segments[2 * n1, rows, :], segments[2 * n1 + 1, rows, :]
                if n1:
                    cos, sin = twiddle_ref[2 * n1], twiddle_ref[2 * n1 + 1]
                    re, im = re * cos + im * sin, im * cos - re * sin
                values.append((re, im))
            values = dft16(values)
            centre = middles[rows, :]
            centre = centre + roll_lanes(centre, -16)
            squares = []
            for g in range(GROUPS):
                for side in range(2):
                    re, im = values[15 - g] if side else values[g]
                    if side:
                        re = jnp.where(lane == 0, roll_lanes(centre, -g), re)
                        im = jnp.where(lane == 0, roll_lanes(centre, -(GROUPS + g)), im)
                    spectrum[4 * g + 2 * side, rows, :] = re
                    spectrum[4 * g + 2 * side + 1, rows, :] = im
                    squares.append(re * re + im * im)
            powers.append(squares)
        both = pl.ds(pl.multiple_of(pair * 16, 16), 16)
        for tile in range(2 * GROUPS):
            joined = jnp.concatenate([powers[0][tile], powers[1][tile]], axis=0)
            power[both, pl.ds((tile + 1) * LANES, LANES)] = joined.astype(jnp.bfloat16)
        return carry

    lax.fori_loop(0, SEGS // 16, combine, 0)

    for g in range(GROUPS):
        smooth[...] = jnp.dot(
            power[:, g * 256 : g * 256 + 512], box_ref[...], preferred_element_type=jnp.float32
        )
        for side in range(2):
            inverse = inverse_ref[2 * g + side]
            for c in range(2):
                sums = None
                for octet in range(NWIN // 8):
                    white = []
                    for o in range(NOFF):
                        rows = pl.ds((2 * o + c) * NWIN + octet * 8, 8)
                        level = smooth[rows, side * LANES : (side + 1) * LANES] * inverse
                        scale = lax.rsqrt(level + epsilon)
                        re = spectrum[4 * g + 2 * side, rows, :] * scale
                        im = spectrum[4 * g + 2 * side + 1, rows, :] * scale
                        white.append((re, im))
                    own_re, own_im = white[0]
                    terms = [own_re * own_re + own_im * own_im]
                    for far_re, far_im in white[1:]:
                        terms.append(own_re * far_re + own_im * far_im)
                        if side:
                            terms.append(own_re * far_im - own_im * far_re)
                        else:
                            terms.append(own_im * far_re - own_re * far_im)
                    sums = terms if sums is None else [a + b for a, b in zip(sums, terms)]
                sums = [jnp.sum(x, axis=0, keepdims=True) * (1.0 / NWIN) for x in sums]
                real = jnp.concatenate([sums[0], sums[1], sums[3], sums[5]], axis=0)
                nothing = jnp.zeros((1, LANES), jnp.float32)
                imag = jnp.concatenate([nothing, sums[2], sums[4], sums[6]], axis=0)
                if side:
                    folded[pl.ds((g * 2 + c) * 8, 4), :] = real
                    folded[pl.ds((g * 2 + c) * 8 + 4, 4), :] = imag
                else:
                    out_ref[c, :, pl.ds(g * 256, LANES)] = real
                    out_ref[c, :, pl.ds(NF + g * 256, LANES)] = imag
    folded[...] = jnp.dot(
        folded[...],
        flip_ref[...],
        preferred_element_type=jnp.float32,
        precision=lax.Precision.HIGHEST,
    )
    for g in range(GROUPS):
        for c in range(2):
            row = (g * 2 + c) * 8
            out_ref[c, :, pl.ds(g * 256 + LANES, LANES)] = folded[pl.ds(row, 4), :]
            out_ref[c, :, pl.ds(NF + g * 256 + LANES, LANES)] = folded[pl.ds(row + 4, 4), :]


def stack(parts, starts):
    shards = parts.shape[0]
    vmem = pl.BlockSpec(memory_space=pltpu.VMEM)
    f32 = jnp.float32
    return pl.pallas_call(
        stack_kernel,
        out_shape=jax.ShapeDtypeStruct((2, NOFF, 2 * NF), f32),
        in_specs=[pl.BlockSpec(memory_space=pltpu.SMEM)] + [vmem] * 8,
        out_specs=vmem,
        scratch_shapes=[
            pltpu.VMEM((shards, ROWS * PHASES, LANES), f32),
            pltpu.VMEM((PHASES, shards, ROWS, LANES), f32),
            pltpu.VMEM((PHASES, shards, ROWS, LANES), f32),
            pltpu.VMEM((PHASES, shards + 1, ROWS, LANES), f32),
            pltpu.VMEM((2 * PHASES, SEGS, LANES), f32),
            pltpu.VMEM((SEGS, LANES), f32),
            pltpu.VMEM((4 * GROUPS, SEGS, LANES), f32),
            pltpu.VMEM((SEGS, (2 * GROUPS + 2) * LANES), jnp.bfloat16),
            pltpu.VMEM((SEGS, 2 * LANES), f32),
            pltpu.VMEM((2 * GROUPS * 8, LANES), f32),
        ],
        compiler_params=pltpu.CompilerParams(vmem_limit_bytes=40 * 1024 * 1024),
    )(starts, parts, *[jnp.asarray(table) for table in tables()])


def ahead_on(array, axis, by):
    size = lax.axis_size(axis)
    return lax.ppermute(array, axis, [((i + by) % size, i) for i in range(size)])


def body(records, dead_flags, starts, offsets):
    rows = records.shape[0]
    dealt = deal(records, dead_flags)
    reach = lax.axis_size("loop") // 2
    blocks = [dealt] + [ahead_on(dealt, "loop", by) for by in range(1, reach + 1)]
    nearby = jnp.concatenate(blocks, axis=0)
    members = lax.axis_size("chan")
    picked = [
        lax.dynamic_slice_in_dim(nearby, offsets[o], rows, 0).reshape(
            members, rows // members, PHASES, LANES
        )
        for o in range(NOFF)
    ]
    outgoing = jnp.concatenate(picked, axis=1)
    parts = lax.all_to_all(outgoing, "chan", split_axis=0, concat_axis=0, tiled=True)
    return stack(parts, starts)


def solution(mesh):
    in_specs = (P("loop", "chan"), P("loop"), P(), P())
    out_specs = P(("loop", "chan"), None, None)
    return jax.shard_map(body, mesh=mesh, in_specs=in_specs, out_specs=out_specs, check_vma=False)
```

time: 528 us -> 58.9 us (0.11); the launches traced: 520 us -> 58.5 us
  other arithmetic: 208 us -> 0.07 us
  waiting for transfers between devices: 140 us -> 0.01 us
  local copies, waits for them, and re-layouts: 107 us -> 4.06 us
  starting transfers between devices: 33 us -> 10.7 us
  Pallas kernels: 0 us -> 19.7 us
  matrix products: 17 us -> 0 us
  blocking collectives: 0 us -> 16.1 us
  between operations: 15.3 us -> 7.91 us
    cos x7 -> x0, other arithmetic: 126 us -> none  [spectra(): jnp.cos(phase_angle)]
    unnamed x2 -> x0, waiting for transfers between devices: 126 us -> none
    gather x101 -> x0, local copies, waits for them, and re-layouts: 80.4 us -> none
    reduce_sum x1 -> x0, other arithmetic: 37.4 us -> none  [add_pairs(): cross_real = jnp.sum(own_real * far_real + own_imag * far_imag, axis=0)]
    pallas_call x0 -> x2, Pallas kernels: none -> 19.7 us  [the longest x1 19.1 us: stack(): pl.pallas_call(stack_kernel, out_shape=jax.ShapeDtypeStruct((2, NOFF, 2 *...]
    neg x1 -> x0, other arithmetic: 17.8 us -> none  [spectra(): -jnp.sin(phase_angle)]
    unnamed x56 -> x28, local copies, waits for them, and re-layouts: 20.5 us -> 3.23 us
    dot_general x16 -> x0, matrix products: 17 us -> none  [the longest x8 10.3 us: spectra(): product = jnp.dot(segments, table_high, preferred_element_type=jnp.float32)]
  transfers between devices with their start and end apart: 9 -> 4, of which waited for: 3 -> 0; matrix products, arithmetic and copies ran while one was open for 37% -> 1% of each run, Pallas kernels for 0% -> 0%
where the time goes in v1:
time: 58.9 us; the launch traced here: 58.5 us
  Pallas kernels  19.7 us (33%)
  blocking collectives  16.1 us (27%)
  starting transfers between devices  10.7 us (18%)
  between operations  7.91 us (13%)
  local copies, waits for them, and re-layouts  4.06 us (7%)
    pallas_call x1, Pallas kernels, stack(): pl.pallas_call(stack_kernel, out_shape=jax.ShapeDtypeStruct((2, NOFF, 2 *...  19.1 us
    all_to_all x1, blocking collectives, body(): lax.all_to_all(outgoing, 'chan', split_axis=0, concat_axis=0, tiled=True)  16.1 us
    ppermute x4, starting transfers between devices, ahead_on(): lax.ppermute(array, axis, [((i + by) % size, i) for i in range(size)])  10.7 us
    unnamed x28, local copies, waits for them, and re-layouts  3.23 us
  transfers between devices with their start and end apart: 4, of which 0 were waited for; matrix products, arithmetic and copies ran while one was open for 1% of the time, Pallas kernels for 0%

profile of v1, /device:TPU:1, one launch (start us, length us, event | category | flops | bytes accessed | tf_op | source)
XLA Modules:
  0.0 58.5 jit_solution(1375256678973329640)
XLA Ops:
  0.0 0.0 copy-start.11
  0.0 0.7 %copy-done.11 = s32[32]{0:T(128)S(1)} copy-done((s32[32]{0:T(128)S(1)}, s32[32]{0:T(128)}, u32[]{:S(2)}) %copy-start.11) | copy-done | bytes 152
  0.7 0.1 copy.13.dead_ref
  0.7 0.0 copy-start.2
  0.7 0.9 %copy-done.2 = bf16[32,2048]{1,0:T(8,128)(2,1)S(1)} copy-done((bf16[32,2048]{1,0:T(8,128)(2,1)S(1)}, bf16[32,2048]{1,0:T(8,128)(2,1)}, u32[]{:S(2)}) %copy-start.2) | copy-done | bytes 131096
  1.6 0.0 copy-start.3
  1.7 0.9 %copy-done.3 = bf16[256,256]{1,0:T(8,128)(2,1)S(1)} copy-done((bf16[256,256]{1,0:T(8,128)(2,1)S(1)}, bf16[256,256]{1,0:T(8,128)(2,1)}, u32[]{:S(2)}) %copy-start.3) | copy-done | bytes 131096
  2.6 0.6 shard_map.118
  3.1 6.9 %collective-permute-start = (bf16[32,16,128]{2,1,0:T(8,128)(2,1)S(1)}, bf16[32,16,128]{2,1,0:T(8,128)(2,1)S(1)}, u32[]{:S(2)}, u32[]{:S(2)}) collective-permute-start(bf16[32,16,128]{2,1,0:T(8,128)(2,1)S(1)} %shard_map.118), channel_id=1, source_target_pairs={{16,0},{32,16},{48,32},{64,48},{80,64},{96,80},{112,96},{0,112},{1... | collective-permute-start | bytes 393224 | tf_op jit(solution)/shard_map/ppermute | solution.py:399
  10.1 0.3 collective-permute-start.1
  10.4 0.0 collective-permute-start.2
  10.4 3.4 %collective-permute-start.3 = (bf16[32,16,128]{2,1,0:T(8,128)(2,1)S(1)}, bf16[32,16,128]{2,1,0:T(8,128)(2,1)S(1)}, u32[]{:S(2)}, u32[]{:S(2)}) collective-permute-start(bf16[32,16,128]{2,1,0:T(8,128)(2,1)S(1)} %shard_map.118), channel_id=1, source_target_pairs={{64,0},{80,16},{96,32},{112,48},{0,64},{16,80},{32,96},{48,112},{6... | collective-permute-start | bytes 393224 | tf_op jit(solution)/shard_map/ppermute | solution.py:399
  13.8 0.0 copy-start.10
  13.8 0.6 %copy-done.10 = s32[4]{0:T(128)S(1)} copy-done((s32[4]{0:T(128)S(1)}, s32[4]{0:T(128)}, u32[]{:S(2)}) %copy-start.10) | copy-done | bytes 40
  14.4 0.7 %fusion = (s32[1]{0:T(128)}, s32[1]{0:T(128)}, s32[1]{0:T(128)}, s32[1]{0:T(128)}) fusion(s32[4]{0:T(128)S(1)} %copy-done.10), kind=kLoop, calls=%fused_computation.10 | loop fusion | bytes 32 | tf_op jit(solution)/shard_map/slice | solution.py:410
  22.8 0.0 collective-permute-done
  22.9 0.0 collective-permute-done.1
  22.9 0.0 collective-permute-done.2
  22.9 0.0 collective-permute-done.3
  23.0 0.1 constant_dynamic-slice_fusion.3
  23.0 0.0 copy-start
  23.1 0.1 pad_maximum_fusion
  23.1 0.0 copy-start.1
  23.1 0.0 copy-start.4
  23.2 0.0 copy-start.5
  23.2 0.0 copy-start.6
  23.2 0.0 copy-start.7
  23.2 0.0 copy-start.8
  23.2 0.0 copy-start.9
  23.2 16.1 %all_to_all.5.parts_ref = bf16[16,8,16,128]{3,2,1,0:T(8,128)(2,1)S(1)} all-to-all(bf16[16,8,16,128]{3,2,1,0:T(8,128)(2,1)S(1)} %pad_maximum_fusion), channel_id=1, replica_groups=mesh['loop'=8,'chan'=16] {'chan'}, dimensions={0} | all-to-all | bytes 1048576 | tf_op jit(solution)/shard_map/all_to_all | solution.py:416
  39.3 0.0 copy-done
  39.3 0.0 copy-done.1
  39.3 0.0 copy-done.4
  39.3 0.0 copy-done.5
  39.4 0.0 copy-done.6
  39.4 0.0 copy-done.7
  39.4 0.0 copy-done.8
  39.4 0.0 copy-done.9
  39.4 19.1 %shard_map.119 = f32[2,4,4096]{2,1,0:T(4,128)} custom-call(s32[32]{0:T(128)S(1)} %copy-done.9, bf16[16,8,16,128]{3,2,1,0:T(8,128)(2,1)S(1)} %all_to_all.5.parts_ref, bf16[256,256]{1,0:T(8,128)(2,1)S(1)} %copy-done.4, bf16[256,256]{1,0:T(8,128)(2,1)S(1)} %copy-done.5, f32[32,8,128]{2,1,0:T(8,128)S(1)} %copy-done.6, bf16[16,256,128]{2,1,0:T(8,128)(2,1)S(1)} %copy-done, ...), custom_call_target="tpu_custom_call" | custom-call | tf_op jit(solution)/shard_map/pallas_call | solution.py:376
  (5 shorter events, 0.1 us)
Async XLA Ops:
  0.0 0.7 %copy-start.11 = (s32[32]{0:T(128)S(1)}, s32[32]{0:T(128)}, u32[]{:S(2)}) copy-start(s32[32]{0:T(128)} %param.13) | copy-start | bytes 388
  0.7 0.9 %copy-start.2 = (bf16[32,2048]{1,0:T(8,128)(2,1)S(1)}, bf16[32,2048]{1,0:T(8,128)(2,1)}, u32[]{:S(2)}) copy-start(bf16[32,2048]{1,0:T(8,128)(2,1)} %records_ref.1) | copy-start | bytes 393220
  1.6 0.9 %copy-start.3 = (bf16[256,256]{1,0:T(8,128)(2,1)S(1)}, bf16[256,256]{1,0:T(8,128)(2,1)}, u32[]{:S(2)}) copy-start(bf16[256,256]{1,0:T(8,128)(2,1)} %constant.20.clone.table_ref) | copy-start | bytes 393220
  3.1 19.7 %collective-permute-start = (bf16[32,16,128]{2,1,0:T(8,128)(2,1)S(1)}, bf16[32,16,128]{2,1,0:T(8,128)(2,1)S(1)}, u32[]{:S(2)}, u32[]{:S(2)}) collective-permute-start(bf16[32,16,128]{2,1,0:T(8,128)(2,1)S(1)} %shard_map.118), channel_id=1, source_target_pairs={{16,0},{32,16},{48,32},{64,48},{80,64},{96,80},{112,96},{0,112},{1... | collective-permute-start | bytes 393224 | tf_op jit(solution)/shard_map/ppermute | solution.py:399
  10.1 12.8 %collective-permute-start.1 = (bf16[32,16,128]{2,1,0:T(8,128)(2,1)S(1)}, bf16[32,16,128]{2,1,0:T(8,128)(2,1)S(1)}, u32[]{:S(2)}, u32[]{:S(2)}) collective-permute-start(bf16[32,16,128]{2,1,0:T(8,128)(2,1)S(1)} %shard_map.118), channel_id=1, source_target_pairs={{32,0},{48,16},{64,32},{80,48},{96,64},{112,80},{0,96},{16,112},{3... | collective-permute-start | bytes 393224 | tf_op jit(solution)/shard_map/ppermute | solution.py:399
  10.4 12.5 %collective-permute-start.2 = (bf16[32,16,128]{2,1,0:T(8,128)(2,1)S(1)}, bf16[32,16,128]{2,1,0:T(8,128)(2,1)S(1)}, u32[]{:S(2)}, u32[]{:S(2)}) collective-permute-start(bf16[32,16,128]{2,1,0:T(8,128)(2,1)S(1)} %shard_map.118), channel_id=1, source_target_pairs={{48,0},{64,16},{80,32},{96,48},{112,64},{0,80},{16,96},{32,112},{4... | collective-permute-start | bytes 393224 | tf_op jit(solution)/shard_map/ppermute | solution.py:399
  10.4 12.5 %collective-permute-start.3 = (bf16[32,16,128]{2,1,0:T(8,128)(2,1)S(1)}, bf16[32,16,128]{2,1,0:T(8,128)(2,1)S(1)}, u32[]{:S(2)}, u32[]{:S(2)}) collective-permute-start(bf16[32,16,128]{2,1,0:T(8,128)(2,1)S(1)} %shard_map.118), channel_id=1, source_target_pairs={{64,0},{80,16},{96,32},{112,48},{0,64},{16,80},{32,96},{48,112},{6... | collective-permute-start | bytes 393224 | tf_op jit(solution)/shard_map/ppermute | solution.py:399
  13.8 0.7 %copy-start.10 = (s32[4]{0:T(128)S(1)}, s32[4]{0:T(128)}, u32[]{:S(2)}) copy-start(s32[4]{0:T(128)} %param.15) | copy-start | bytes 52
  23.0 16.3 %copy-start = (bf16[16,256,128]{2,1,0:T(8,128)(2,1)S(1)}, bf16[16,256,128]{2,1,0:T(8,128)(2,1)}, u32[]{:S(2)}) copy-start(bf16[16,256,128]{2,1,0:T(8,128)(2,1)} %constant.24.clone.middle_ref) | copy-start | bytes 3145732
  23.1 16.2 %copy-start.1 = (bf16[512,256]{1,0:T(8,128)(2,1)S(1)}, bf16[512,256]{1,0:T(8,128)(2,1)}, u32[]{:S(2)}) copy-start(bf16[512,256]{1,0:T(8,128)(2,1)} %constant.25.clone.box_ref) | copy-start | bytes 786436
  23.1 16.2 %copy-start.4 = (bf16[256,256]{1,0:T(8,128)(2,1)S(1)}, bf16[256,256]{1,0:T(8,128)(2,1)}, u32[]{:S(2)}) copy-start(bf16[256,256]{1,0:T(8,128)(2,1)} %constant.21.clone.high_ref) | copy-start | bytes 393220
  23.2 16.2 %copy-start.5 = (bf16[256,256]{1,0:T(8,128)(2,1)S(1)}, bf16[256,256]{1,0:T(8,128)(2,1)}, u32[]{:S(2)}) copy-start(bf16[256,256]{1,0:T(8,128)(2,1)} %constant.22.clone.low_ref) | copy-start | bytes 393220
  23.2 16.2 %copy-start.6 = (f32[32,8,128]{2,1,0:T(8,128)S(1)}, f32[32,8,128]{2,1,0:T(8,128)}, u32[]{:S(2)}) copy-start(f32[32,8,128]{2,1,0:T(8,128)} %constant.23.clone.twiddle_ref) | copy-start | bytes 393220
  23.2 16.2 %copy-start.7 = (f32[16,8,128]{2,1,0:T(8,128)S(1)}, f32[16,8,128]{2,1,0:T(8,128)}, u32[]{:S(2)}) copy-start(f32[16,8,128]{2,1,0:T(8,128)} %constant.26.clone.inverse_ref) | copy-start | bytes 196612
  23.2 16.2 %copy-start.8 = (f32[128,128]{1,0:T(8,128)S(1)}, f32[128,128]{1,0:T(8,128)}, u32[]{:S(2)}) copy-start(f32[128,128]{1,0:T(8,128)} %constant.27.clone.flip_ref) | copy-start | bytes 196612
  23.2 16.2 %copy-start.9 = (s32[32]{0:T(128)S(1)}, s32[32]{0:T(128)}, u32[]{:S(2)}) copy-start(s32[32]{0:T(128)} %starts_ref.1) | copy-start | bytes 388

commit v2 on v1

--- a/solution.py
+++ b/solution.py
@@ -19,6 +19,7 @@
 WIN = 4096
 LANES = 128
 PHASES = 16
+PITCH = PHASES + 1
 ROWS = 8
 SEGS = ROWS * NWIN
 GROUPS = NF // 256
@@ -71,14 +72,6 @@
     return first_high, first_low, twiddle, middle, box, inverse, flip
 
 
-@functools.lru_cache(maxsize=None)
-def deal_table():
-    column = np.arange(256)
-    table = np.zeros((256, 256), ml_dtypes.bfloat16)
-    table[(column % 16) * 16 + column // 16, column] = 1.0
-    return table
-
-
 def lane_index(rows=ROWS):
     return lax.broadcasted_iota(jnp.int32, (rows, LANES), 1)
 
@@ -87,15 +80,21 @@
     return pltpu.roll(value, by % LANES, 1)
 
 
-def deal_kernel(records_ref, dead_ref, table_ref, out_ref, staged):
+def deal_kernel(records_ref, dead_ref, out_ref, staged):
     rows = records_ref.shape[0]
+    place = lax.broadcasted_iota(jnp.int32, (rows, rows), 0)
+    across = lax.broadcasted_iota(jnp.int32, (rows, rows), 1)
     live = (1 - dead_ref[...]).astype(jnp.float32)
+    live = jnp.sum(jnp.where(place == across, live, 0.0), axis=1, keepdims=True)
+    source = lax.broadcasted_iota(jnp.int32, (256, 256), 0)
+    target = lax.broadcasted_iota(jnp.int32, (256, 256), 1)
+    table = (source == (target % 16) * 16 + target // 16).astype(jnp.bfloat16)
     lane = lane_index(rows)
     parts = [[None] * 8, [None] * 8]
     for chunk in range(8):
         product = jnp.dot(
             records_ref[:, chunk * 256 : (chunk + 1) * 256],
-            table_ref[...],
+            table,
             preferred_element_type=jnp.float32,
         )
         parts[0][chunk] = product[:, :LANES]
@@ -113,8 +112,9 @@
                     following[index | bit] = jnp.where(keep, roll_lanes(low, -step), high)
             current = following
         for index in range(8):
-            staged[pl.ds(half * 8 + index, rows, stride=PHASES), :] = current[index] * live
-    out_ref[...] = staged[...].reshape(rows, PHASES, LANES).astype(jnp.bfloat16)
+            staged[pl.ds(half * 8 + index, rows, stride=PITCH), :] = current[index] * live
+    for r in range(rows):
+        out_ref[r] = staged[pl.ds(r * PITCH, PHASES), :].astype(jnp.bfloat16)
 
 
 def deal(records, dead_flags):
@@ -123,11 +123,11 @@
     return pl.pallas_call(
         deal_kernel,
         out_shape=jax.ShapeDtypeStruct((rows, PHASES, LANES), jnp.bfloat16),
-        in_specs=[vmem] * 3,
+        in_specs=[vmem] * 2,
         out_specs=vmem,
-        scratch_shapes=[pltpu.VMEM((rows * PHASES, LANES), jnp.float32)],
+        scratch_shapes=[pltpu.VMEM((rows * PITCH, LANES), jnp.float32)],
         compiler_params=pltpu.CompilerParams(vmem_limit_bytes=16 * 1024 * 1024),
-    )(records, dead_flags.reshape(rows, 1), jnp.asarray(deal_table()))
+    )(records, dead_flags.reshape(1, rows))
 
 
 def dft4(a, b, c, d):
@@ -179,6 +179,8 @@
     after,
     normed,
     segments,
+    samples,
+    factor,
     middles,
     spectrum,
     power,
@@ -187,12 +189,14 @@
 ):
     lane = lane_index()
     shards = parts_ref.shape[0]
-    plain[...] = parts_ref[...].reshape(shards, ROWS * PHASES, LANES).astype(jnp.float32)
+    for k in range(shards):
+        for r in range(ROWS):
+            plain[k, pl.ds(r * PITCH, PHASES), :] = parts_ref[k, r].astype(jnp.float32)
 
     totals = []
     for k in range(shards):
         level = [
-            jnp.abs(plain[k, pl.ds(p, ROWS, stride=PHASES), :]) for p in range(PHASES)
+            jnp.abs(plain[k, pl.ds(p, ROWS, stride=PITCH), :]) for p in range(PHASES)
         ]
         running = jnp.zeros((ROWS, LANES), jnp.float32)
         for p in range(PHASES):
@@ -229,6 +233,7 @@
     def normalize(p, carry):
         first = behind([after[p, k] for k in range(shards)], 8)
         last = ahead([before[p, k] for k in range(shards)], 8)
+        tiles = []
         for k in range(shards):
             full = smooth[pl.ds(k * ROWS, ROWS), pl.ds(0, LANES)]
             total = full + first[k] + last[k]
@@ -238,50 +243,49 @@
                 mean_level = total / count.astype(jnp.float32)
             else:
                 mean_level = total * (1.0 / RMW)
-            signal = plain[k, pl.ds(p, ROWS, stride=PHASES), :]
+            signal = plain[k, pl.ds(p, ROWS, stride=PITCH), :]
             ratio = signal / (mean_level + epsilon)
-            normed[p, k] = ratio.astype(jnp.bfloat16).astype(jnp.float32)
+            tiles.append(ratio.astype(jnp.bfloat16).astype(jnp.float32))
+        for k, (tile, later) in enumerate(zip(tiles, ahead(tiles, 1))):
+            normed[p, k] = tile
+            normed[p + PHASES, k] = later
         normed[p, shards] = zero
+        normed[p + PHASES, shards] = zero
         return carry
 
-    lax.fori_loop(0, PHASES, normalize, 0)
+    lax.fori_loop(0, PHASES, normalize, 0, unroll=4)
 
     def cut(w, carry):
         start = starts_ref[w]
         phase = start & (PHASES - 1)
         column = start >> 4
+        tile = column >> 7
+        by = column & (LANES - 1)
+        keep = lane >= by
+        turn = (LANES - by) & (LANES - 1)
         for n1 in range(PHASES):
-            place = phase + n1
-            here = column + (place >> 4)
-            tile = here >> 7
-            by = here & (LANES - 1)
-            p = place & (PHASES - 1)
-            a, b, c = normed[p, tile], normed[p, tile + 1], normed[p, tile + 2]
-            keep = lane >= by
-            turn = (LANES - by) & (LANES - 1)
-            segments[2 * n1, pl.ds(w, ROWS, stride=NWIN), :] = pltpu.roll(
-                jnp.where(keep, a, b), turn, 1
+            a, b, c = [normed[phase + n1, tile + step] for step in range(3)]
+            for half, joined in enumerate((jnp.where(keep, a, b), jnp.where(keep, b, c))):
+                rows = pl.ds(w, ROWS, stride=NWIN + 1)
+                segments[2 * n1 + half, rows, :] = pltpu.roll(joined, turn, 1)
+        return carry
+
+    lax.fori_loop(0, NWIN, cut, 0, unroll=4)
+
+    for n1 in range(PHASES):
+        for r in range(ROWS):
+            both = jnp.concatenate(
+                [segments[2 * n1 + h, pl.ds(r * (NWIN + 1), NWIN), :] for h in range(2)], axis=1
             )
-            segments[2 * n1 + 1, pl.ds(w, ROWS, stride=NWIN), :] = pltpu.roll(
-                jnp.where(keep, b, c), turn, 1
-            )
-        return carry
-
-    lax.fori_loop(0, NWIN, cut, 0)
-
-    middles[...] = jnp.zeros_like(middles)
-
-    def transform(n1, carry):
-        left = jnp.concatenate([segments[2 * n1], segments[2 * n1 + 1]], axis=1)
-        left = left.astype(jnp.bfloat16)
-        product = jnp.dot(left, high_ref[...], preferred_element_type=jnp.float32)
-        product = product + jnp.dot(left, low_ref[...], preferred_element_type=jnp.float32)
-        middles[...] += jnp.dot(left, middle_ref[n1], preferred_element_type=jnp.float32)
-        segments[2 * n1] = product[:, :LANES]
-        segments[2 * n1 + 1] = product[:, LANES:]
-        return carry
-
-    lax.fori_loop(0, PHASES, transform, 0)
+            samples[n1, pl.ds(r * NWIN, NWIN), :] = both.astype(jnp.bfloat16)
+    left = samples[...].reshape(PHASES * SEGS, 2 * LANES)
+    product = jnp.dot(left, high_ref[...], preferred_element_type=jnp.float32)
+    product = product + jnp.dot(left, low_ref[...], preferred_element_type=jnp.float32)
+    factor[...] = product.reshape(PHASES, SEGS, 2 * LANES)
+    left = jnp.concatenate([samples[n1] for n1 in range(PHASES)], axis=1)
+    middles[...] = jnp.dot(
+        left, middle_ref[...].reshape(WIN, LANES), preferred_element_type=jnp.float32
+    )
 
     zero_pair = jnp.zeros((SEGS, LANES), jnp.bfloat16)
     power[:, pl.ds(0, LANES)] = zero_pair
@@ -293,7 +297,7 @@
             rows = pl.ds(pl.multiple_of(pair * 16 + part * ROWS, ROWS), ROWS)
             values = []
             for n1 in range(PHASES):
-                re, im = segments[2 * n1, rows, :], segments[2 * n1 + 1, rows, :]
+                re, im = factor[n1, rows, pl.ds(0, LANES)], factor[n1, rows, pl.ds(LANES, LANES)]
                 if n1:
                     cos, sin = twiddle_ref[2 * n1], twiddle_ref[2 * n1 + 1]
                     re, im = re * cos + im * sin, im * cos - re * sin
@@ -318,7 +322,7 @@
             power[both, pl.ds((tile + 1) * LANES, LANES)] = joined.astype(jnp.bfloat16)
         return carry
 
-    lax.fori_loop(0, SEGS // 16, combine, 0)
+    lax.fori_loop(0, SEGS // 16, combine, 0, unroll=4)
 
     for g in range(GROUPS):
         smooth[...] = jnp.dot(
@@ -379,11 +383,13 @@
         in_specs=[pl.BlockSpec(memory_space=pltpu.SMEM)] + [vmem] * 8,
         out_specs=vmem,
         scratch_shapes=[
-            pltpu.VMEM((shards, ROWS * PHASES, LANES), f32),
+            pltpu.VMEM((shards, ROWS * PITCH, LANES), f32),
             pltpu.VMEM((PHASES, shards, ROWS, LANES), f32),
             pltpu.VMEM((PHASES, shards, ROWS, LANES), f32),
-            pltpu.VMEM((PHASES, shards + 1, ROWS, LANES), f32),
-            pltpu.VMEM((2 * PHASES, SEGS, LANES), f32),
+            pltpu.VMEM((2 * PHASES, shards + 1, ROWS, LANES), f32),
+            pltpu.VMEM((2 * PHASES, ROWS * (NWIN + 1), LANES), f32),
+            pltpu.VMEM((PHASES, SEGS, 2 * LANES), jnp.bfloat16),
+            pltpu.VMEM((PHASES, SEGS, 2 * LANES), f32),
             pltpu.VMEM((SEGS, LANES), f32),
             pltpu.VMEM((4 * GROUPS, SEGS, LANES), f32),
             pltpu.VMEM((SEGS, (2 * GROUPS + 2) * LANES), jnp.bfloat16),

time: 58.9 us -> 49.3 us (0.84)
  Pallas kernels: 19.7 us -> 11.2 us
  local copies, waits for them, and re-layouts: 4.06 us -> 3.05 us
    pallas_call x1, Pallas kernels: 19.1 us -> 10.6 us  [stack(): pl.pallas_call(stack_kernel, out_shape=jax.ShapeDtypeStruct((2, NOFF, 2 *...]
    unnamed x28 -> x26, local copies, waits for them, and re-layouts: 3.23 us -> 2.32 us
where the time goes in v2:
time: 49.3 us; the launch traced here: 48.9 us
  blocking collectives  16.1 us (33%)
  Pallas kernels  11.2 us (23%)
  starting transfers between devices  10.7 us (22%)
  between operations  7.75 us (16%)
  local copies, waits for them, and re-layouts  3.05 us (6%)
    all_to_all x1, blocking collectives, body(): lax.all_to_all(outgoing, 'chan', split_axis=0, concat_axis=0, tiled=True)  16.1 us
    ppermute x4, starting transfers between devices, ahead_on(): lax.ppermute(array, axis, [((i + by) % size, i) for i in range(size)])  10.7 us
    pallas_call x1, Pallas kernels, stack(): pl.pallas_call(stack_kernel, out_shape=jax.ShapeDtypeStruct((2, NOFF, 2 *...  10.6 us
    unnamed x26, local copies, waits for them, and re-layouts  2.32 us
  transfers between devices with their start and end apart: 4, of which 0 were waited for; matrix products, arithmetic and copies ran while one was open for 1% of the time, Pallas kernels for 0%

profile of v2, /device:TPU:1, one launch (start us, length us, event | category | flops | bytes accessed | tf_op | source)
XLA Modules:
  0.0 48.9 jit_solution(2728429697737217676)
XLA Ops:
  0.0 0.0 copy-start.8
  0.0 0.7 %copy-done.8 = s32[32]{0:T(128)S(1)} copy-done((s32[32]{0:T(128)S(1)}, s32[32]{0:T(128)}, u32[]{:S(2)}) %copy-start.8) | copy-done | bytes 152
  0.7 0.0 copy-start.2
  0.7 0.9 %copy-done.2 = bf16[32,2048]{1,0:T(8,128)(2,1)S(1)} copy-done((bf16[32,2048]{1,0:T(8,128)(2,1)S(1)}, bf16[32,2048]{1,0:T(8,128)(2,1)}, u32[]{:S(2)}) %copy-start.2) | copy-done | bytes 131096
  1.6 0.6 %shard_map.109 = bf16[32,16,128]{2,1,0:T(8,128)(2,1)S(1)} custom-call(bf16[32,2048]{1,0:T(8,128)(2,1)S(1)} %copy-done.2, s32[1,32]{1,0:T(1,128)S(1)} %bitcast.9), custom_call_target="tpu_custom_call" | custom-call | tf_op jit(solution)/shard_map/pallas_call | solution.py:123
  2.1 6.9 %collective-permute-start = (bf16[32,16,128]{2,1,0:T(8,128)(2,1)S(1)}, bf16[32,16,128]{2,1,0:T(8,128)(2,1)S(1)}, u32[]{:S(2)}, u32[]{:S(2)}) collective-permute-start(bf16[32,16,128]{2,1,0:T(8,128)(2,1)S(1)} %shard_map.109), channel_id=1, source_target_pairs={{16,0},{32,16},{48,32},{64,48},{80,64},{96,80},{112,96},{0,112},{1... | collective-permute-start | bytes 393224 | tf_op jit(solution)/shard_map/ppermute | solution.py:405
  9.1 0.3 collective-permute-start.1
  9.4 0.0 collective-permute-start.2
  9.4 3.4 %collective-permute-start.3 = (bf16[32,16,128]{2,1,0:T(8,128)(2,1)S(1)}, bf16[32,16,128]{2,1,0:T(8,128)(2,1)S(1)}, u32[]{:S(2)}, u32[]{:S(2)}) collective-permute-start(bf16[32,16,128]{2,1,0:T(8,128)(2,1)S(1)} %shard_map.109), channel_id=1, source_target_pairs={{64,0},{80,16},{96,32},{112,48},{0,64},{16,80},{32,96},{48,112},{6... | collective-permute-start | bytes 393224 | tf_op jit(solution)/shard_map/ppermute | solution.py:405
  12.8 0.0 copy-start.10
  12.8 0.6 %copy-done.10 = s32[4]{0:T(128)S(1)} copy-done((s32[4]{0:T(128)S(1)}, s32[4]{0:T(128)}, u32[]{:S(2)}) %copy-start.10) | copy-done | bytes 40
  13.4 0.7 %fusion = (s32[1]{0:T(128)}, s32[1]{0:T(128)}, s32[1]{0:T(128)}, s32[1]{0:T(128)}) fusion(s32[4]{0:T(128)S(1)} %copy-done.10), kind=kLoop, calls=%fused_computation.10 | loop fusion | bytes 32 | tf_op jit(solution)/shard_map/slice | solution.py:416
  21.7 0.0 collective-permute-done
  21.7 0.0 collective-permute-done.1
  21.7 0.0 collective-permute-done.2
  21.8 0.0 collective-permute-done.3
  21.9 0.0 copy-start
  21.9 0.1 pad_maximum_fusion
  21.9 0.0 copy-start.1
  22.0 0.0 copy-start.3
  22.0 0.0 copy-start.4
  22.0 0.0 copy-start.5
  22.0 0.0 copy-start.6
  22.0 0.0 copy-start.7
  22.0 0.0 copy-start.9
  22.0 16.1 %all_to_all.5.parts_ref = bf16[16,8,16,128]{3,2,1,0:T(8,128)(2,1)S(1)} all-to-all(bf16[16,8,16,128]{3,2,1,0:T(8,128)(2,1)S(1)} %pad_maximum_fusion), channel_id=1, replica_groups=mesh['loop'=8,'chan'=16] {'chan'}, dimensions={0} | all-to-all | bytes 1048576 | tf_op jit(solution)/shard_map/all_to_all | solution.py:422
  38.2 0.0 copy-done
  38.2 0.0 copy-done.1
  38.2 0.0 copy-done.3
  38.2 0.0 copy-done.4
  38.2 0.0 copy-done.5
  38.2 0.0 copy-done.6
  38.2 0.0 copy-done.7
  38.2 0.0 copy-done.9
  38.2 10.6 %shard_map.110 = f32[2,4,4096]{2,1,0:T(4,128)} custom-call(s32[32]{0:T(128)S(1)} %copy-done.9, bf16[16,8,16,128]{3,2,1,0:T(8,128)(2,1)S(1)} %all_to_all.5.parts_ref, bf16[256,256]{1,0:T(8,128)(2,1)S(1)} %copy-done.3, bf16[256,256]{1,0:T(8,128)(2,1)S(1)} %copy-done.4, f32[32,8,128]{2,1,0:T(8,128)S(1)} %copy-done.5, bf16[16,256,128]{2,1,0:T(8,128)(2,1)S(1)} %copy-done, ...), custom_call_target="tpu_custom_call" | custom-call | tf_op jit(solution)/shard_map/pallas_call | solution.py:380
  (6 shorter events, 0.1 us)
Async XLA Ops:
  0.0 0.7 %copy-start.8 = (s32[32]{0:T(128)S(1)}, s32[32]{0:T(128)}, u32[]{:S(2)}) copy-start(s32[32]{0:T(128)} %param.12) | copy-start | bytes 388
  0.7 0.9 %copy-start.2 = (bf16[32,2048]{1,0:T(8,128)(2,1)S(1)}, bf16[32,2048]{1,0:T(8,128)(2,1)}, u32[]{:S(2)}) copy-start(bf16[32,2048]{1,0:T(8,128)(2,1)} %records_ref.1) | copy-start | bytes 393220
  2.1 19.5 %collective-permute-start = (bf16[32,16,128]{2,1,0:T(8,128)(2,1)S(1)}, bf16[32,16,128]{2,1,0:T(8,128)(2,1)S(1)}, u32[]{:S(2)}, u32[]{:S(2)}) collective-permute-start(bf16[32,16,128]{2,1,0:T(8,128)(2,1)S(1)} %shard_map.109), channel_id=1, source_target_pairs={{16,0},{32,16},{48,32},{64,48},{80,64},{96,80},{112,96},{0,112},{1... | collective-permute-start | bytes 393224 | tf_op jit(solution)/shard_map/ppermute | solution.py:405
  9.1 12.6 %collective-permute-start.1 = (bf16[32,16,128]{2,1,0:T(8,128)(2,1)S(1)}, bf16[32,16,128]{2,1,0:T(8,128)(2,1)S(1)}, u32[]{:S(2)}, u32[]{:S(2)}) collective-permute-start(bf16[32,16,128]{2,1,0:T(8,128)(2,1)S(1)} %shard_map.109), channel_id=1, source_target_pairs={{32,0},{48,16},{64,32},{80,48},{96,64},{112,80},{0,96},{16,112},{3... | collective-permute-start | bytes 393224 | tf_op jit(solution)/shard_map/ppermute | solution.py:405
  9.4 12.3 %collective-permute-start.2 = (bf16[32,16,128]{2,1,0:T(8,128)(2,1)S(1)}, bf16[32,16,128]{2,1,0:T(8,128)(2,1)S(1)}, u32[]{:S(2)}, u32[]{:S(2)}) collective-permute-start(bf16[32,16,128]{2,1,0:T(8,128)(2,1)S(1)} %shard_map.109), channel_id=1, source_target_pairs={{48,0},{64,16},{80,32},{96,48},{112,64},{0,80},{16,96},{32,112},{4... | collective-permute-start | bytes 393224 | tf_op jit(solution)/shard_map/ppermute | solution.py:405
  9.4 12.4 %collective-permute-start.3 = (bf16[32,16,128]{2,1,0:T(8,128)(2,1)S(1)}, bf16[32,16,128]{2,1,0:T(8,128)(2,1)S(1)}, u32[]{:S(2)}, u32[]{:S(2)}) collective-permute-start(bf16[32,16,128]{2,1,0:T(8,128)(2,1)S(1)} %shard_map.109), channel_id=1, source_target_pairs={{64,0},{80,16},{96,32},{112,48},{0,64},{16,80},{32,96},{48,112},{6... | collective-permute-start | bytes 393224 | tf_op jit(solution)/shard_map/ppermute | solution.py:405
  12.8 0.7 %copy-start.10 = (s32[4]{0:T(128)S(1)}, s32[4]{0:T(128)}, u32[]{:S(2)}) copy-start(s32[4]{0:T(128)} %param.14) | copy-start | bytes 52
  21.9 16.3 %copy-start = (bf16[16,256,128]{2,1,0:T(8,128)(2,1)S(1)}, bf16[16,256,128]{2,1,0:T(8,128)(2,1)}, u32[]{:S(2)}) copy-start(bf16[16,256,128]{2,1,0:T(8,128)(2,1)} %constant.21.clone.middle_ref) | copy-start | bytes 3145732
  21.9 16.2 %copy-start.1 = (bf16[512,256]{1,0:T(8,128)(2,1)S(1)}, bf16[512,256]{1,0:T(8,128)(2,1)}, u32[]{:S(2)}) copy-start(bf16[512,256]{1,0:T(8,128)(2,1)} %constant.22.clone.box_ref) | copy-start | bytes 786436
  22.0 16.2 %copy-start.3 = (bf16[256,256]{1,0:T(8,128)(2,1)S(1)}, bf16[256,256]{1,0:T(8,128)(2,1)}, u32[]{:S(2)}) copy-start(bf16[256,256]{1,0:T(8,128)(2,1)} %constant.18.clone.high_ref) | copy-start | bytes 393220
  22.0 16.2 %copy-start.4 = (bf16[256,256]{1,0:T(8,128)(2,1)S(1)}, bf16[256,256]{1,0:T(8,128)(2,1)}, u32[]{:S(2)}) copy-start(bf16[256,256]{1,0:T(8,128)(2,1)} %constant.19.clone.low_ref) | copy-start | bytes 393220
  22.0 16.2 %copy-start.5 = (f32[32,8,128]{2,1,0:T(8,128)S(1)}, f32[32,8,128]{2,1,0:T(8,128)}, u32[]{:S(2)}) copy-start(f32[32,8,128]{2,1,0:T(8,128)} %constant.20.clone.twiddle_ref) | copy-start | bytes 393220
  22.0 16.2 %copy-start.6 = (f32[16,8,128]{2,1,0:T(8,128)S(1)}, f32[16,8,128]{2,1,0:T(8,128)}, u32[]{:S(2)}) copy-start(f32[16,8,128]{2,1,0:T(8,128)} %constant.23.clone.inverse_ref) | copy-start | bytes 196612
  22.0 16.2 %copy-start.7 = (f32[128,128]{1,0:T(8,128)S(1)}, f32[128,128]{1,0:T(8,128)}, u32[]{:S(2)}) copy-start(f32[128,128]{1,0:T(8,128)} %constant.24.clone.flip_ref) | copy-start | bytes 196612
  22.0 16.2 %copy-start.9 = (s32[32]{0:T(128)S(1)}, s32[32]{0:T(128)}, u32[]{:S(2)}) copy-start(s32[32]{0:T(128)} %starts_ref.1) | copy-start | bytes 388

commit v3 on v2

--- a/solution.py
+++ b/solution.py
@@ -69,7 +69,10 @@
 
     flip = np.zeros((LANES, LANES), np.float32)
     flip[(LANES - lane) % LANES, lane] = 1.0
-    return first_high, first_low, twiddle, middle, box, inverse, flip
+    row = np.arange(2 * LANES)[:, None]
+    shift = np.concatenate([row == 120 + lane[None, :], row == 8 + lane[None, :]], axis=1)
+    shift = shift.astype(ml_dtypes.bfloat16)
+    return shift, first_high, first_low, twiddle, middle, box, inverse, flip
 
 
 def lane_index(rows=ROWS):
@@ -80,15 +83,23 @@
     return pltpu.roll(value, by % LANES, 1)
 
 
-def deal_kernel(records_ref, dead_ref, out_ref, staged):
-    rows = records_ref.shape[0]
+def deal_kernel(records_hbm, dead_hbm, out_ref, records_ref, dead_ref, staged, sems):
+    rows = records_hbm.shape[0]
+    copies = [
+        pltpu.make_async_copy(dead_hbm, dead_ref, sems.at[0]),
+        pltpu.make_async_copy(records_hbm, records_ref, sems.at[1]),
+    ]
+    for copy in copies:
+        copy.start()
+    source = lax.broadcasted_iota(jnp.int32, (256, 256), 0)
+    target = lax.broadcasted_iota(jnp.int32, (256, 256), 1)
+    table = (source == (target % 16) * 16 + target // 16).astype(jnp.bfloat16)
+    copies[0].wait()
     place = lax.broadcasted_iota(jnp.int32, (rows, rows), 0)
     across = lax.broadcasted_iota(jnp.int32, (rows, rows), 1)
     live = (1 - dead_ref[...]).astype(jnp.float32)
     live = jnp.sum(jnp.where(place == across, live, 0.0), axis=1, keepdims=True)
-    source = lax.broadcasted_iota(jnp.int32, (256, 256), 0)
-    target = lax.broadcasted_iota(jnp.int32, (256, 256), 1)
-    table = (source == (target % 16) * 16 + target // 16).astype(jnp.bfloat16)
+    copies[1].wait()
     lane = lane_index(rows)
     parts = [[None] * 8, [None] * 8]
     for chunk in range(8):
@@ -118,14 +129,18 @@
 
 
 def deal(records, dead_flags):
-    rows = records.shape[0]
-    vmem = pl.BlockSpec(memory_space=pltpu.VMEM)
+    rows, length = records.shape
     return pl.pallas_call(
         deal_kernel,
         out_shape=jax.ShapeDtypeStruct((rows, PHASES, LANES), jnp.bfloat16),
-        in_specs=[vmem] * 2,
-        out_specs=vmem,
-        scratch_shapes=[pltpu.VMEM((rows * PITCH, LANES), jnp.float32)],
+        in_specs=[pl.BlockSpec(memory_space=pl.ANY)] * 2,
+        out_specs=pl.BlockSpec(memory_space=pltpu.VMEM),
+        scratch_shapes=[
+            pltpu.VMEM((rows, length), jnp.bfloat16),
+            pltpu.VMEM((1, rows), jnp.int32),
+            pltpu.VMEM((rows * PITCH, LANES), jnp.float32),
+            pltpu.SemaphoreType.DMA((2,)),
+        ],
         compiler_params=pltpu.CompilerParams(vmem_limit_bytes=16 * 1024 * 1024),
     )(records, dead_flags.reshape(1, rows))
 
@@ -166,6 +181,7 @@
 def stack_kernel(
     starts_ref,
     parts_ref,
+    shift_ref,
     high_ref,
     low_ref,
     twiddle_ref,
@@ -175,8 +191,8 @@
     flip_ref,
     out_ref,
     plain,
-    before,
-    after,
+    levels,
+    moved,
     normed,
     segments,
     samples,
@@ -193,20 +209,18 @@
         for r in range(ROWS):
             plain[k, pl.ds(r * PITCH, PHASES), :] = parts_ref[k, r].astype(jnp.float32)
 
+    none = jnp.zeros((PHASES * ROWS, LANES), jnp.bfloat16)
+    levels[0] = none
+    levels[shards + 1] = none
     totals = []
     for k in range(shards):
-        level = [
-            jnp.abs(plain[k, pl.ds(p, ROWS, stride=PITCH), :]) for p in range(PHASES)
-        ]
-        running = jnp.zeros((ROWS, LANES), jnp.float32)
-        for p in range(PHASES):
-            before[p, k] = running
-            running = running + level[p]
-        totals.append(running)
-        running = jnp.zeros((ROWS, LANES), jnp.float32)
-        for p in reversed(range(PHASES)):
-            running = running + level[p]
-            after[p, k] = running
+        level = [jnp.abs(plain[k, pl.ds(p, ROWS, stride=PITCH), :]) for p in range(PHASES)]
+        totals.append(functools.reduce(lambda a, b: a + b, level))
+        levels[k + 1] = jnp.concatenate(level, axis=0).astype(jnp.bfloat16)
+    pairs = jnp.concatenate([levels[: shards + 1], levels[1:]], axis=2)
+    pairs = pairs.reshape((shards + 1) * PHASES * ROWS, 2 * LANES)
+    product = jnp.dot(pairs, shift_ref[...], preferred_element_type=jnp.float32)
+    moved[...] = product.reshape(shards + 1, PHASES * ROWS, 2 * LANES)
     zero = jnp.zeros((ROWS, LANES), jnp.float32)
 
     def ahead(tiles, by):
@@ -228,15 +242,15 @@
         past = plus(past, behind(past, by))
     columns = plus(columns, past)
     for k in range(shards):
-        smooth[pl.ds(k * ROWS, ROWS), pl.ds(0, LANES)] = columns[k]
-
-    def normalize(p, carry):
-        first = behind([after[p, k] for k in range(shards)], 8)
-        last = ahead([before[p, k] for k in range(shards)], 8)
-        tiles = []
-        for k in range(shards):
-            full = smooth[pl.ds(k * ROWS, ROWS), pl.ds(0, LANES)]
-            total = full + first[k] + last[k]
+        running = zero
+        after = [None] * PHASES
+        for p in reversed(range(PHASES)):
+            running = running + moved[k, pl.ds(p * ROWS, ROWS), pl.ds(0, LANES)]
+            after[p] = running
+        running = columns[k]
+        for p in range(PHASES):
+            total = running + after[p]
+            running = running + moved[k + 1, pl.ds(p * ROWS, ROWS), pl.ds(LANES, LANES)]
             if k in (0, shards - 1):
                 place = p + PHASES * (k * LANES + lane)
                 count = jnp.minimum(place + RMW // 2, NT) - jnp.maximum(place - RMW // 2, 0)
@@ -245,29 +259,20 @@
                 mean_level = total * (1.0 / RMW)
             signal = plain[k, pl.ds(p, ROWS, stride=PITCH), :]
             ratio = signal / (mean_level + epsilon)
-            tiles.append(ratio.astype(jnp.bfloat16).astype(jnp.float32))
-        for k, (tile, later) in enumerate(zip(tiles, ahead(tiles, 1))):
-            normed[p, k] = tile
-            normed[p + PHASES, k] = later
-        normed[p, shards] = zero
-        normed[p + PHASES, shards] = zero
-        return carry
-
-    lax.fori_loop(0, PHASES, normalize, 0, unroll=4)
+            normed[p, k] = ratio.astype(jnp.bfloat16).astype(jnp.float32)
 
     def cut(w, carry):
         start = starts_ref[w]
         phase = start & (PHASES - 1)
         column = start >> 4
-        tile = column >> 7
-        by = column & (LANES - 1)
-        keep = lane >= by
-        turn = (LANES - by) & (LANES - 1)
-        for n1 in range(PHASES):
-            a, b, c = [normed[phase + n1, tile + step] for step in range(3)]
-            for half, joined in enumerate((jnp.where(keep, a, b), jnp.where(keep, b, c))):
-                rows = pl.ds(w, ROWS, stride=NWIN + 1)
-                segments[2 * n1 + half, rows, :] = pltpu.roll(joined, turn, 1)
+        tile = (column >> 8) * 2
+        first = column & 255
+        for p in range(PHASES):
+            least = first + (p < phase).astype(jnp.int32)
+            for half in range(2):
+                keep = lane >= least - half * LANES
+                joined = jnp.where(keep, normed[p, tile + half], normed[p, tile + 2 + half])
+                segments[2 * p + half, pl.ds(w, ROWS, stride=NWIN + 1), :] = joined
         return carry
 
     lax.fori_loop(0, NWIN, cut, 0, unroll=4)
@@ -380,13 +385,13 @@
     return pl.pallas_call(
         stack_kernel,
         out_shape=jax.ShapeDtypeStruct((2, NOFF, 2 * NF), f32),
-        in_specs=[pl.BlockSpec(memory_space=pltpu.SMEM)] + [vmem] * 8,
+        in_specs=[pl.BlockSpec(memory_space=pltpu.SMEM)] + [vmem] * 9,
         out_specs=vmem,
         scratch_shapes=[
             pltpu.VMEM((shards, ROWS * PITCH, LANES), f32),
-            pltpu.VMEM((PHASES, shards, ROWS, LANES), f32),
-            pltpu.VMEM((PHASES, shards, ROWS, LANES), f32),
-            pltpu.VMEM((2 * PHASES, shards + 1, ROWS, LANES), f32),
+            pltpu.VMEM((shards + 2, PHASES * ROWS, LANES), jnp.bfloat16),
+            pltpu.VMEM((shards + 1, PHASES * ROWS, 2 * LANES), f32),
+            pltpu.VMEM((PHASES, shards + 2, ROWS, LANES), f32),
             pltpu.VMEM((2 * PHASES, ROWS * (NWIN + 1), LANES), f32),
             pltpu.VMEM((PHASES, SEGS, 2 * LANES), jnp.bfloat16),
             pltpu.VMEM((PHASES, SEGS, 2 * LANES), f32),

time: 49.3 us -> 47.7 us (0.968)
  Pallas kernels: 11.2 us -> 9.38 us
    pallas_call x1, Pallas kernels: 10.6 us -> 8.58 us  [stack(): pl.pallas_call(stack_kernel, out_shape=jax.ShapeDtypeStruct((2, NOFF, 2 *...]
    unnamed x26 -> x28, local copies, waits for them, and re-layouts: 2.32 us -> 2.33 us
  transfers between devices with their start and end apart: 4 -> 4, of which waited for: 0 -> 0; matrix products, arithmetic and copies ran while one was open for 1% -> 2% of each run, Pallas kernels for 0% -> 0%
where the time goes in v3:
time: 47.7 us; the launch traced here: 47.2 us
  blocking collectives  16.1 us (34%)
  starting transfers between devices  10.7 us (22%)
  Pallas kernels  9.38 us (20%)
  between operations  7.93 us (17%)
  local copies, waits for them, and re-layouts  3.08 us (6%)
    all_to_all x1, blocking collectives, body(): lax.all_to_all(outgoing, 'chan', split_axis=0, concat_axis=0, tiled=True)  16.1 us
    ppermute x4, starting transfers between devices, ahead_on(): lax.ppermute(array, axis, [((i + by) % size, i) for i in range(size)])  10.7 us
    pallas_call x1, Pallas kernels, stack(): pl.pallas_call(stack_kernel, out_shape=jax.ShapeDtypeStruct((2, NOFF, 2 *...  8.58 us
    unnamed x28, local copies, waits for them, and re-layouts  2.33 us
  transfers between devices with their start and end apart: 4, of which 0 were waited for; matrix products, arithmetic and copies ran while one was open for 2% of the time, Pallas kernels for 0%

profile of v3, /device:TPU:1, one launch (start us, length us, event | category | flops | bytes accessed | tf_op | source)
XLA Modules:
  0.0 47.2 jit_solution(15809824268573171527)
XLA Ops:
  0.0 0.0 copy-start.9
  0.0 0.7 %copy-done.9 = s32[32]{0:T(128)S(1)} copy-done((s32[32]{0:T(128)S(1)}, s32[32]{0:T(128)}, u32[]{:S(2)}) %copy-start.9) | copy-done | bytes 152
  0.7 0.0 copy-start.6
  0.7 0.9 %copy-done.6 = bf16[32,2048]{1,0:T(8,128)(2,1)S(1)} copy-done((bf16[32,2048]{1,0:T(8,128)(2,1)S(1)}, bf16[32,2048]{1,0:T(8,128)(2,1)}, u32[]{:S(2)}) %copy-start.6) | copy-done | bytes 131096
  1.6 0.8 %shard_map.118 = bf16[32,16,128]{2,1,0:T(8,128)(2,1)S(1)} custom-call(bf16[32,2048]{1,0:T(8,128)(2,1)S(1)} %copy-done.6, s32[1,32]{1,0:T(1,128)S(1)} %bitcast.9), custom_call_target="tpu_custom_call" | custom-call | tf_op jit(solution)/shard_map/pallas_call | solution.py:133
  2.4 6.9 %collective-permute-start = (bf16[32,16,128]{2,1,0:T(8,128)(2,1)S(1)}, bf16[32,16,128]{2,1,0:T(8,128)(2,1)S(1)}, u32[]{:S(2)}, u32[]{:S(2)}) collective-permute-start(bf16[32,16,128]{2,1,0:T(8,128)(2,1)S(1)} %shard_map.118), channel_id=1, source_target_pairs={{16,0},{32,16},{48,32},{64,48},{80,64},{96,80},{112,96},{0,112},{1... | collective-permute-start | bytes 393224 | tf_op jit(solution)/shard_map/ppermute | solution.py:410
  9.3 0.3 collective-permute-start.1
  9.7 0.0 collective-permute-start.2
  9.7 3.4 %collective-permute-start.3 = (bf16[32,16,128]{2,1,0:T(8,128)(2,1)S(1)}, bf16[32,16,128]{2,1,0:T(8,128)(2,1)S(1)}, u32[]{:S(2)}, u32[]{:S(2)}) collective-permute-start(bf16[32,16,128]{2,1,0:T(8,128)(2,1)S(1)} %shard_map.118), channel_id=1, source_target_pairs={{64,0},{80,16},{96,32},{112,48},{0,64},{16,80},{32,96},{48,112},{6... | collective-permute-start | bytes 393224 | tf_op jit(solution)/shard_map/ppermute | solution.py:410
  13.0 0.0 copy-start.11
  13.1 0.6 %copy-done.11 = s32[4]{0:T(128)S(1)} copy-done((s32[4]{0:T(128)S(1)}, s32[4]{0:T(128)}, u32[]{:S(2)}) %copy-start.11) | copy-done | bytes 40
  13.7 0.7 %fusion = (s32[1]{0:T(128)}, s32[1]{0:T(128)}, s32[1]{0:T(128)}, s32[1]{0:T(128)}) fusion(s32[4]{0:T(128)S(1)} %copy-done.11), kind=kLoop, calls=%fused_computation.10 | loop fusion | bytes 32 | tf_op jit(solution)/shard_map/slice | solution.py:421
  22.1 0.0 collective-permute-done
  22.1 0.0 collective-permute-done.1
  22.2 0.0 collective-permute-done.2
  22.2 0.0 collective-permute-done.3
  22.2 0.1 constant_dynamic-slice_fusion.3
  22.3 0.0 copy-start
  22.3 0.1 pad_maximum_fusion
  22.4 0.0 copy-start.1
  22.4 0.0 copy-start.2
  22.4 0.0 copy-start.3
  22.4 0.0 copy-start.4
  22.4 0.0 copy-start.5
  22.4 0.0 copy-start.7
  22.5 0.0 copy-start.8
  22.5 0.0 copy-start.10
  22.5 16.1 %all_to_all.5.parts_ref = bf16[16,8,16,128]{3,2,1,0:T(8,128)(2,1)S(1)} all-to-all(bf16[16,8,16,128]{3,2,1,0:T(8,128)(2,1)S(1)} %pad_maximum_fusion), channel_id=1, replica_groups=mesh['loop'=8,'chan'=16] {'chan'}, dimensions={0} | all-to-all | bytes 1048576 | tf_op jit(solution)/shard_map/all_to_all | solution.py:427
  38.6 0.0 copy-done
  38.6 0.0 copy-done.1
  38.6 0.0 copy-done.2
  38.6 0.0 copy-done.3
  38.6 0.0 copy-done.4
  38.6 0.0 copy-done.5
  38.6 0.0 copy-done.7
  38.7 0.0 copy-done.8
  38.7 0.0 copy-done.10
  38.7 8.6 %shard_map.119 = f32[2,4,4096]{2,1,0:T(4,128)} custom-call(s32[32]{0:T(128)S(1)} %copy-done.10, bf16[16,8,16,128]{3,2,1,0:T(8,128)(2,1)S(1)} %all_to_all.5.parts_ref, bf16[256,256]{1,0:T(8,128)(2,1)S(1)} %copy-done.2, bf16[256,256]{1,0:T(8,128)(2,1)S(1)} %copy-done.3, bf16[256,256]{1,0:T(8,128)(2,1)S(1)} %copy-done.4, f32[32,8,128]{2,1,0:T(8,128)S(1)} %copy-done.5, ...), custom_call_target="tpu_custom_call" | custom-call | tf_op jit(solution)/shard_map/pallas_call | solution.py:385
  (5 shorter events, 0.1 us)
Async XLA Ops:
  0.0 0.7 %copy-start.9 = (s32[32]{0:T(128)S(1)}, s32[32]{0:T(128)}, u32[]{:S(2)}) copy-start(s32[32]{0:T(128)} %param.13) | copy-start | bytes 388
  0.7 0.9 %copy-start.6 = (bf16[32,2048]{1,0:T(8,128)(2,1)S(1)}, bf16[32,2048]{1,0:T(8,128)(2,1)}, u32[]{:S(2)}) copy-start(bf16[32,2048]{1,0:T(8,128)(2,1)} %records_hbm.1) | copy-start | bytes 393220
  2.4 19.7 %collective-permute-start = (bf16[32,16,128]{2,1,0:T(8,128)(2,1)S(1)}, bf16[32,16,128]{2,1,0:T(8,128)(2,1)S(1)}, u32[]{:S(2)}, u32[]{:S(2)}) collective-permute-start(bf16[32,16,128]{2,1,0:T(8,128)(2,1)S(1)} %shard_map.118), channel_id=1, source_target_pairs={{16,0},{32,16},{48,32},{64,48},{80,64},{96,80},{112,96},{0,112},{1... | collective-permute-start | bytes 393224 | tf_op jit(solution)/shard_map/ppermute | solution.py:410
  9.3 12.8 %collective-permute-start.1 = (bf16[32,16,128]{2,1,0:T(8,128)(2,1)S(1)}, bf16[32,16,128]{2,1,0:T(8,128)(2,1)S(1)}, u32[]{:S(2)}, u32[]{:S(2)}) collective-permute-start(bf16[32,16,128]{2,1,0:T(8,128)(2,1)S(1)} %shard_map.118), channel_id=1, source_target_pairs={{32,0},{48,16},{64,32},{80,48},{96,64},{112,80},{0,96},{16,112},{3... | collective-permute-start | bytes 393224 | tf_op jit(solution)/shard_map/ppermute | solution.py:410
  9.7 12.5 %collective-permute-start.2 = (bf16[32,16,128]{2,1,0:T(8,128)(2,1)S(1)}, bf16[32,16,128]{2,1,0:T(8,128)(2,1)S(1)}, u32[]{:S(2)}, u32[]{:S(2)}) collective-permute-start(bf16[32,16,128]{2,1,0:T(8,128)(2,1)S(1)} %shard_map.118), channel_id=1, source_target_pairs={{48,0},{64,16},{80,32},{96,48},{112,64},{0,80},{16,96},{32,112},{4... | collective-permute-start | bytes 393224 | tf_op jit(solution)/shard_map/ppermute | solution.py:410
  9.7 12.5 %collective-permute-start.3 = (bf16[32,16,128]{2,1,0:T(8,128)(2,1)S(1)}, bf16[32,16,128]{2,1,0:T(8,128)(2,1)S(1)}, u32[]{:S(2)}, u32[]{:S(2)}) collective-permute-start(bf16[32,16,128]{2,1,0:T(8,128)(2,1)S(1)} %shard_map.118), channel_id=1, source_target_pairs={{64,0},{80,16},{96,32},{112,48},{0,64},{16,80},{32,96},{48,112},{6... | collective-permute-start | bytes 393224 | tf_op jit(solution)/shard_map/ppermute | solution.py:410
  13.0 0.7 %copy-start.11 = (s32[4]{0:T(128)S(1)}, s32[4]{0:T(128)}, u32[]{:S(2)}) copy-start(s32[4]{0:T(128)} %param.15) | copy-start | bytes 52
  22.3 16.3 %copy-start = (bf16[16,256,128]{2,1,0:T(8,128)(2,1)S(1)}, bf16[16,256,128]{2,1,0:T(8,128)(2,1)}, u32[]{:S(2)}) copy-start(bf16[16,256,128]{2,1,0:T(8,128)(2,1)} %constant.24.clone.middle_ref) | copy-start | bytes 3145732
  22.4 16.2 %copy-start.1 = (bf16[512,256]{1,0:T(8,128)(2,1)S(1)}, bf16[512,256]{1,0:T(8,128)(2,1)}, u32[]{:S(2)}) copy-start(bf16[512,256]{1,0:T(8,128)(2,1)} %constant.25.clone.box_ref) | copy-start | bytes 786436
  22.4 16.2 %copy-start.2 = (bf16[256,256]{1,0:T(8,128)(2,1)S(1)}, bf16[256,256]{1,0:T(8,128)(2,1)}, u32[]{:S(2)}) copy-start(bf16[256,256]{1,0:T(8,128)(2,1)} %constant.20.clone.shift_ref) | copy-start | bytes 393220
  22.4 16.2 %copy-start.3 = (bf16[256,256]{1,0:T(8,128)(2,1)S(1)}, bf16[256,256]{1,0:T(8,128)(2,1)}, u32[]{:S(2)}) copy-start(bf16[256,256]{1,0:T(8,128)(2,1)} %constant.21.clone.high_ref) | copy-start | bytes 393220
  22.4 16.2 %copy-start.4 = (bf16[256,256]{1,0:T(8,128)(2,1)S(1)}, bf16[256,256]{1,0:T(8,128)(2,1)}, u32[]{:S(2)}) copy-start(bf16[256,256]{1,0:T(8,128)(2,1)} %constant.22.clone.low_ref) | copy-start | bytes 393220
  22.4 16.2 %copy-start.5 = (f32[32,8,128]{2,1,0:T(8,128)S(1)}, f32[32,8,128]{2,1,0:T(8,128)}, u32[]{:S(2)}) copy-start(f32[32,8,128]{2,1,0:T(8,128)} %constant.23.clone.twiddle_ref) | copy-start | bytes 393220
  22.4 16.2 %copy-start.7 = (f32[16,8,128]{2,1,0:T(8,128)S(1)}, f32[16,8,128]{2,1,0:T(8,128)}, u32[]{:S(2)}) copy-start(f32[16,8,128]{2,1,0:T(8,128)} %constant.26.clone.inverse_ref) | copy-start | bytes 196612
  22.5 16.2 %copy-start.8 = (f32[128,128]{1,0:T(8,128)S(1)}, f32[128,128]{1,0:T(8,128)}, u32[]{:S(2)}) copy-start(f32[128,128]{1,0:T(8,128)} %constant.27.clone.flip_ref) | copy-start | bytes 196612
  22.5 16.2 %copy-start.10 = (s32[32]{0:T(128)S(1)}, s32[32]{0:T(128)}, u32[]{:S(2)}) copy-start(s32[32]{0:T(128)} %starts_ref.1) | copy-start | bytes 388

commit v4 on v3

--- a/solution.py
+++ b/solution.py
@@ -133,7 +133,7 @@
     return pl.pallas_call(
         deal_kernel,
         out_shape=jax.ShapeDtypeStruct((rows, PHASES, LANES), jnp.bfloat16),
-        in_specs=[pl.BlockSpec(memory_space=pl.ANY)] * 2,
+        in_specs=[pl.BlockSpec(memory_space=pltpu.HBM)] * 2,
         out_specs=pl.BlockSpec(memory_space=pltpu.VMEM),
         scratch_shapes=[
             pltpu.VMEM((rows, length), jnp.bfloat16),
@@ -202,6 +202,7 @@
     power,
     smooth,
     folded,
+    turned,
 ):
     lane = lane_index()
     shards = parts_ref.shape[0]
@@ -261,16 +262,15 @@
             ratio = signal / (mean_level + epsilon)
             normed[p, k] = ratio.astype(jnp.bfloat16).astype(jnp.float32)
 
+    place = lane * PHASES
+
     def cut(w, carry):
         start = starts_ref[w]
-        phase = start & (PHASES - 1)
-        column = start >> 4
-        tile = (column >> 8) * 2
-        first = column & 255
+        tile = (start >> 12) * 2
+        first = start & (WIN - 1)
         for p in range(PHASES):
-            least = first + (p < phase).astype(jnp.int32)
             for half in range(2):
-                keep = lane >= least - half * LANES
+                keep = place >= first - (half * LANES * PHASES + p)
                 joined = jnp.where(keep, normed[p, tile + half], normed[p, tile + 2 + half])
                 segments[2 * p + half, pl.ds(w, ROWS, stride=NWIN + 1), :] = joined
         return carry
@@ -283,10 +283,11 @@
                 [segments[2 * n1 + h, pl.ds(r * (NWIN + 1), NWIN), :] for h in range(2)], axis=1
             )
             samples[n1, pl.ds(r * NWIN, NWIN), :] = both.astype(jnp.bfloat16)
-    left = samples[...].reshape(PHASES * SEGS, 2 * LANES)
-    product = jnp.dot(left, high_ref[...], preferred_element_type=jnp.float32)
-    product = product + jnp.dot(left, low_ref[...], preferred_element_type=jnp.float32)
-    factor[...] = product.reshape(PHASES, SEGS, 2 * LANES)
+    for n1 in range(0, PHASES, 4):
+        left = samples[n1 : n1 + 4].reshape(4 * SEGS, 2 * LANES)
+        product = jnp.dot(left, high_ref[...], preferred_element_type=jnp.float32)
+        product = product + jnp.dot(left, low_ref[...], preferred_element_type=jnp.float32)
+        factor[n1 : n1 + 4] = product.reshape(4, SEGS, 2 * LANES)
     left = jnp.concatenate([samples[n1] for n1 in range(PHASES)], axis=1)
     middles[...] = jnp.dot(
         left, middle_ref[...].reshape(WIN, LANES), preferred_element_type=jnp.float32
@@ -330,7 +331,7 @@
     lax.fori_loop(0, SEGS // 16, combine, 0, unroll=4)
 
     for g in range(GROUPS):
-        smooth[...] = jnp.dot(
+        smooth[g] = jnp.dot(
             power[:, g * 256 : g * 256 + 512], box_ref[...], preferred_element_type=jnp.float32
         )
         for side in range(2):
@@ -341,7 +342,7 @@
                     white = []
                     for o in range(NOFF):
                         rows = pl.ds((2 * o + c) * NWIN + octet * 8, 8)
-                        level = smooth[rows, side * LANES : (side + 1) * LANES] * inverse
+                        level = smooth[g, rows, pl.ds(side * LANES, LANES)] * inverse
                         scale = lax.rsqrt(level + epsilon)
                         re = spectrum[4 * g + 2 * side, rows, :] * scale
                         im = spectrum[4 * g + 2 * side + 1, rows, :] * scale
@@ -355,16 +356,17 @@
                         else:
                             terms.append(own_im * far_re - own_re * far_im)
                     sums = terms if sums is None else [a + b for a, b in zip(sums, terms)]
-                sums = [jnp.sum(x, axis=0, keepdims=True) * (1.0 / NWIN) for x in sums]
-                real = jnp.concatenate([sums[0], sums[1], sums[3], sums[5]], axis=0)
-                nothing = jnp.zeros((1, LANES), jnp.float32)
-                imag = jnp.concatenate([nothing, sums[2], sums[4], sums[6]], axis=0)
+                place = (2 * g + side) * 2 + c
+                rows = [sums[0], sums[1], sums[3], sums[5], zero, sums[2], sums[4], sums[6]]
+                for index, value in enumerate(rows):
+                    turned[place, pl.ds(index, 8, stride=9), :] = value
+                result = [turned[place, pl.ds(9 * index, 8), :] for index in range(8)]
+                result = functools.reduce(lambda a, b: a + b, result) * (1.0 / NWIN)
                 if side:
-                    folded[pl.ds((g * 2 + c) * 8, 4), :] = real
-                    folded[pl.ds((g * 2 + c) * 8 + 4, 4), :] = imag
+                    folded[pl.ds((g * 2 + c) * 8, 8), :] = result
                 else:
-                    out_ref[c, :, pl.ds(g * 256, LANES)] = real
-                    out_ref[c, :, pl.ds(NF + g * 256, LANES)] = imag
+                    out_ref[c, :, pl.ds(g * 256, LANES)] = result[:NOFF]
+                    out_ref[c, :, pl.ds(NF + g * 256, LANES)] = result[NOFF:]
     folded[...] = jnp.dot(
         folded[...],
         flip_ref[...],
@@ -398,8 +400,9 @@
             pltpu.VMEM((SEGS, LANES), f32),
             pltpu.VMEM((4 * GROUPS, SEGS, LANES), f32),
             pltpu.VMEM((SEGS, (2 * GROUPS + 2) * LANES), jnp.bfloat16),
-            pltpu.VMEM((SEGS, 2 * LANES), f32),
+            pltpu.VMEM((GROUPS, SEGS, 2 * LANES), f32),
             pltpu.VMEM((2 * GROUPS * 8, LANES), f32),
+            pltpu.VMEM((4 * GROUPS, 72, LANES), f32),
         ],
         compiler_params=pltpu.CompilerParams(vmem_limit_bytes=40 * 1024 * 1024),
     )(starts, parts, *[jnp.asarray(table) for table in tables()])

time: 47.7 us -> 47.1 us (0.987)
  Pallas kernels: 9.38 us -> 8.83 us
    pallas_call x1, Pallas kernels: 8.58 us -> 8.03 us  [stack(): pl.pallas_call(stack_kernel, out_shape=jax.ShapeDtypeStruct((2, NOFF, 2 *...]
where the time goes in v4:
time: 47.1 us; the launch traced here: 46.7 us
  blocking collectives  16.1 us (34%)
  starting transfers between devices  10.7 us (23%)
  Pallas kernels  8.83 us (19%)
  between operations  7.93 us (17%)
  local copies, waits for them, and re-layouts  3.08 us (7%)
    all_to_all x1, blocking collectives, body(): lax.all_to_all(outgoing, 'chan', split_axis=0, concat_axis=0, tiled=True)  16.1 us
    ppermute x4, starting transfers between devices, ahead_on(): lax.ppermute(array, axis, [((i + by) % size, i) for i in range(size)])  10.7 us
    pallas_call x1, Pallas kernels, stack(): pl.pallas_call(stack_kernel, out_shape=jax.ShapeDtypeStruct((2, NOFF, 2 *...  8.03 us
    unnamed x28, local copies, waits for them, and re-layouts  2.33 us
  transfers between devices with their start and end apart: 4, of which 0 were waited for; matrix products, arithmetic and copies ran while one was open for 2% of the time, Pallas kernels for 0%

profile of v4, /device:TPU:1, one launch (start us, length us, event | category | flops | bytes accessed | tf_op | source)
XLA Modules:
  0.0 46.7 jit_solution(13195720742206991818)
XLA Ops:
  0.0 0.0 copy-start.9
  0.0 0.7 %copy-done.9 = s32[32]{0:T(128)S(1)} copy-done((s32[32]{0:T(128)S(1)}, s32[32]{0:T(128)}, u32[]{:S(2)}) %copy-start.9) | copy-done | bytes 152
  0.7 0.0 copy-start.6
  0.7 0.9 %copy-done.6 = bf16[32,2048]{1,0:T(8,128)(2,1)S(1)} copy-done((bf16[32,2048]{1,0:T(8,128)(2,1)S(1)}, bf16[32,2048]{1,0:T(8,128)(2,1)}, u32[]{:S(2)}) %copy-start.6) | copy-done | bytes 131096
  1.6 0.8 %shard_map.118 = bf16[32,16,128]{2,1,0:T(8,128)(2,1)S(1)} custom-call(bf16[32,2048]{1,0:T(8,128)(2,1)S(1)} %copy-done.6, s32[1,32]{1,0:T(1,128)S(1)} %bitcast.9), custom_call_target="tpu_custom_call" | custom-call | tf_op jit(solution)/shard_map/pallas_call | solution.py:133
  2.4 6.9 %collective-permute-start = (bf16[32,16,128]{2,1,0:T(8,128)(2,1)S(1)}, bf16[32,16,128]{2,1,0:T(8,128)(2,1)S(1)}, u32[]{:S(2)}, u32[]{:S(2)}) collective-permute-start(bf16[32,16,128]{2,1,0:T(8,128)(2,1)S(1)} %shard_map.118), channel_id=1, source_target_pairs={{16,0},{32,16},{48,32},{64,48},{80,64},{96,80},{112,96},{0,112},{1... | collective-permute-start | bytes 393224 | tf_op jit(solution)/shard_map/ppermute | solution.py:413
  9.3 0.3 collective-permute-start.1
  9.7 0.0 collective-permute-start.2
  9.7 3.4 %collective-permute-start.3 = (bf16[32,16,128]{2,1,0:T(8,128)(2,1)S(1)}, bf16[32,16,128]{2,1,0:T(8,128)(2,1)S(1)}, u32[]{:S(2)}, u32[]{:S(2)}) collective-permute-start(bf16[32,16,128]{2,1,0:T(8,128)(2,1)S(1)} %shard_map.118), channel_id=1, source_target_pairs={{64,0},{80,16},{96,32},{112,48},{0,64},{16,80},{32,96},{48,112},{6... | collective-permute-start | bytes 393224 | tf_op jit(solution)/shard_map/ppermute | solution.py:413
  13.0 0.0 copy-start.11
  13.1 0.6 %copy-done.11 = s32[4]{0:T(128)S(1)} copy-done((s32[4]{0:T(128)S(1)}, s32[4]{0:T(128)}, u32[]{:S(2)}) %copy-start.11) | copy-done | bytes 40
  13.7 0.7 %fusion = (s32[1]{0:T(128)}, s32[1]{0:T(128)}, s32[1]{0:T(128)}, s32[1]{0:T(128)}) fusion(s32[4]{0:T(128)S(1)} %copy-done.11), kind=kLoop, calls=%fused_computation.10 | loop fusion | bytes 32 | tf_op jit(solution)/shard_map/slice | solution.py:424
  22.1 0.0 collective-permute-done
  22.1 0.0 collective-permute-done.1
  22.2 0.0 collective-permute-done.2
  22.2 0.0 collective-permute-done.3
  22.2 0.1 constant_dynamic-slice_fusion.3
  22.3 0.0 copy-start
  22.3 0.1 pad_maximum_fusion
  22.4 0.0 copy-start.1
  22.4 0.0 copy-start.2
  22.4 0.0 copy-start.3
  22.4 0.0 copy-start.4
  22.4 0.0 copy-start.5
  22.4 0.0 copy-start.7
  22.5 0.0 copy-start.8
  22.5 0.0 copy-start.10
  22.5 16.1 %all_to_all.5.parts_ref = bf16[16,8,16,128]{3,2,1,0:T(8,128)(2,1)S(1)} all-to-all(bf16[16,8,16,128]{3,2,1,0:T(8,128)(2,1)S(1)} %pad_maximum_fusion), channel_id=1, replica_groups=mesh['loop'=8,'chan'=16] {'chan'}, dimensions={0} | all-to-all | bytes 1048576 | tf_op jit(solution)/shard_map/all_to_all | solution.py:430
  38.6 0.0 copy-done
  38.6 0.0 copy-done.1
  38.6 0.0 copy-done.2
  38.6 0.0 copy-done.3
  38.6 0.0 copy-done.4
  38.6 0.0 copy-done.5
  38.6 0.0 copy-done.7
  38.7 0.0 copy-done.8
  38.7 0.0 copy-done.10
  38.7 8.0 %shard_map.119 = f32[2,4,4096]{2,1,0:T(4,128)} custom-call(s32[32]{0:T(128)S(1)} %copy-done.10, bf16[16,8,16,128]{3,2,1,0:T(8,128)(2,1)S(1)} %all_to_all.5.parts_ref, bf16[256,256]{1,0:T(8,128)(2,1)S(1)} %copy-done.2, bf16[256,256]{1,0:T(8,128)(2,1)S(1)} %copy-done.3, bf16[256,256]{1,0:T(8,128)(2,1)S(1)} %copy-done.4, f32[32,8,128]{2,1,0:T(8,128)S(1)} %copy-done.5, ...), custom_call_target="tpu_custom_call" | custom-call | tf_op jit(solution)/shard_map/pallas_call | solution.py:387
  (5 shorter events, 0.1 us)
Async XLA Ops:
  0.0 0.7 %copy-start.9 = (s32[32]{0:T(128)S(1)}, s32[32]{0:T(128)}, u32[]{:S(2)}) copy-start(s32[32]{0:T(128)} %param.13) | copy-start | bytes 388
  0.7 0.9 %copy-start.6 = (bf16[32,2048]{1,0:T(8,128)(2,1)S(1)}, bf16[32,2048]{1,0:T(8,128)(2,1)}, u32[]{:S(2)}) copy-start(bf16[32,2048]{1,0:T(8,128)(2,1)} %records_hbm.1) | copy-start | bytes 393220
  2.4 19.7 %collective-permute-start = (bf16[32,16,128]{2,1,0:T(8,128)(2,1)S(1)}, bf16[32,16,128]{2,1,0:T(8,128)(2,1)S(1)}, u32[]{:S(2)}, u32[]{:S(2)}) collective-permute-start(bf16[32,16,128]{2,1,0:T(8,128)(2,1)S(1)} %shard_map.118), channel_id=1, source_target_pairs={{16,0},{32,16},{48,32},{64,48},{80,64},{96,80},{112,96},{0,112},{1... | collective-permute-start | bytes 393224 | tf_op jit(solution)/shard_map/ppermute | solution.py:413
  9.3 12.8 %collective-permute-start.1 = (bf16[32,16,128]{2,1,0:T(8,128)(2,1)S(1)}, bf16[32,16,128]{2,1,0:T(8,128)(2,1)S(1)}, u32[]{:S(2)}, u32[]{:S(2)}) collective-permute-start(bf16[32,16,128]{2,1,0:T(8,128)(2,1)S(1)} %shard_map.118), channel_id=1, source_target_pairs={{32,0},{48,16},{64,32},{80,48},{96,64},{112,80},{0,96},{16,112},{3... | collective-permute-start | bytes 393224 | tf_op jit(solution)/shard_map/ppermute | solution.py:413
  9.7 12.5 %collective-permute-start.2 = (bf16[32,16,128]{2,1,0:T(8,128)(2,1)S(1)}, bf16[32,16,128]{2,1,0:T(8,128)(2,1)S(1)}, u32[]{:S(2)}, u32[]{:S(2)}) collective-permute-start(bf16[32,16,128]{2,1,0:T(8,128)(2,1)S(1)} %shard_map.118), channel_id=1, source_target_pairs={{48,0},{64,16},{80,32},{96,48},{112,64},{0,80},{16,96},{32,112},{4... | collective-permute-start | bytes 393224 | tf_op jit(solution)/shard_map/ppermute | solution.py:413
  9.7 12.5 %collective-permute-start.3 = (bf16[32,16,128]{2,1,0:T(8,128)(2,1)S(1)}, bf16[32,16,128]{2,1,0:T(8,128)(2,1)S(1)}, u32[]{:S(2)}, u32[]{:S(2)}) collective-permute-start(bf16[32,16,128]{2,1,0:T(8,128)(2,1)S(1)} %shard_map.118), channel_id=1, source_target_pairs={{64,0},{80,16},{96,32},{112,48},{0,64},{16,80},{32,96},{48,112},{6... | collective-permute-start | bytes 393224 | tf_op jit(solution)/shard_map/ppermute | solution.py:413
  13.0 0.7 %copy-start.11 = (s32[4]{0:T(128)S(1)}, s32[4]{0:T(128)}, u32[]{:S(2)}) copy-start(s32[4]{0:T(128)} %param.15) | copy-start | bytes 52
  22.3 16.3 %copy-start = (bf16[16,256,128]{2,1,0:T(8,128)(2,1)S(1)}, bf16[16,256,128]{2,1,0:T(8,128)(2,1)}, u32[]{:S(2)}) copy-start(bf16[16,256,128]{2,1,0:T(8,128)(2,1)} %constant.24.clone.middle_ref) | copy-start | bytes 3145732
  22.4 16.2 %copy-start.1 = (bf16[512,256]{1,0:T(8,128)(2,1)S(1)}, bf16[512,256]{1,0:T(8,128)(2,1)}, u32[]{:S(2)}) copy-start(bf16[512,256]{1,0:T(8,128)(2,1)} %constant.25.clone.box_ref) | copy-start | bytes 786436
  22.4 16.2 %copy-start.2 = (bf16[256,256]{1,0:T(8,128)(2,1)S(1)}, bf16[256,256]{1,0:T(8,128)(2,1)}, u32[]{:S(2)}) copy-start(bf16[256,256]{1,0:T(8,128)(2,1)} %constant.20.clone.shift_ref) | copy-start | bytes 393220
  22.4 16.2 %copy-start.3 = (bf16[256,256]{1,0:T(8,128)(2,1)S(1)}, bf16[256,256]{1,0:T(8,128)(2,1)}, u32[]{:S(2)}) copy-start(bf16[256,256]{1,0:T(8,128)(2,1)} %constant.21.clone.high_ref) | copy-start | bytes 393220
  22.4 16.2 %copy-start.4 = (bf16[256,256]{1,0:T(8,128)(2,1)S(1)}, bf16[256,256]{1,0:T(8,128)(2,1)}, u32[]{:S(2)}) copy-start(bf16[256,256]{1,0:T(8,128)(2,1)} %constant.22.clone.low_ref) | copy-start | bytes 393220
  22.4 16.2 %copy-start.5 = (f32[32,8,128]{2,1,0:T(8,128)S(1)}, f32[32,8,128]{2,1,0:T(8,128)}, u32[]{:S(2)}) copy-start(f32[32,8,128]{2,1,0:T(8,128)} %constant.23.clone.twiddle_ref) | copy-start | bytes 393220
  22.4 16.2 %copy-start.7 = (f32[16,8,128]{2,1,0:T(8,128)S(1)}, f32[16,8,128]{2,1,0:T(8,128)}, u32[]{:S(2)}) copy-start(f32[16,8,128]{2,1,0:T(8,128)} %constant.26.clone.inverse_ref) | copy-start | bytes 196612
  22.5 16.2 %copy-start.8 = (f32[128,128]{1,0:T(8,128)S(1)}, f32[128,128]{1,0:T(8,128)}, u32[]{:S(2)}) copy-start(f32[128,128]{1,0:T(8,128)} %constant.27.clone.flip_ref) | copy-start | bytes 196612
  22.5 16.2 %copy-start.10 = (s32[32]{0:T(128)S(1)}, s32[32]{0:T(128)}, u32[]{:S(2)}) copy-start(s32[32]{0:T(128)} %starts_ref.1) | copy-start | bytes 388

commit v5 on v4

--- a/solution.py
+++ b/solution.py
@@ -83,23 +83,15 @@
     return pltpu.roll(value, by % LANES, 1)
 
 
-def deal_kernel(records_hbm, dead_hbm, out_ref, records_ref, dead_ref, staged, sems):
-    rows = records_hbm.shape[0]
-    copies = [
-        pltpu.make_async_copy(dead_hbm, dead_ref, sems.at[0]),
-        pltpu.make_async_copy(records_hbm, records_ref, sems.at[1]),
-    ]
-    for copy in copies:
-        copy.start()
+def deal_kernel(records_ref, live_ref, out_ref, staged):
+    rows = records_ref.shape[0]
     source = lax.broadcasted_iota(jnp.int32, (256, 256), 0)
     target = lax.broadcasted_iota(jnp.int32, (256, 256), 1)
     table = (source == (target % 16) * 16 + target // 16).astype(jnp.bfloat16)
-    copies[0].wait()
     place = lax.broadcasted_iota(jnp.int32, (rows, rows), 0)
     across = lax.broadcasted_iota(jnp.int32, (rows, rows), 1)
-    live = (1 - dead_ref[...]).astype(jnp.float32)
-    live = jnp.sum(jnp.where(place == across, live, 0.0), axis=1, keepdims=True)
-    copies[1].wait()
+    live = jnp.where(place == across, live_ref[...], 0.0)
+    live = jnp.sum(live, axis=1, keepdims=True)
     lane = lane_index(rows)
     parts = [[None] * 8, [None] * 8]
     for chunk in range(8):
@@ -129,20 +121,17 @@
 
 
 def deal(records, dead_flags):
-    rows, length = records.shape
+    rows = records.shape[0]
+    live = (1 - dead_flags).astype(jnp.float32).reshape(1, rows)
+    vmem = pl.BlockSpec(memory_space=pltpu.VMEM)
     return pl.pallas_call(
         deal_kernel,
         out_shape=jax.ShapeDtypeStruct((rows, PHASES, LANES), jnp.bfloat16),
-        in_specs=[pl.BlockSpec(memory_space=pltpu.HBM)] * 2,
-        out_specs=pl.BlockSpec(memory_space=pltpu.VMEM),
-        scratch_shapes=[
-            pltpu.VMEM((rows, length), jnp.bfloat16),
-            pltpu.VMEM((1, rows), jnp.int32),
-            pltpu.VMEM((rows * PITCH, LANES), jnp.float32),
-            pltpu.SemaphoreType.DMA((2,)),
-        ],
+        in_specs=[vmem] * 2,
+        out_specs=vmem,
+        scratch_shapes=[pltpu.VMEM((rows * PITCH, LANES), jnp.float32)],
         compiler_params=pltpu.CompilerParams(vmem_limit_bytes=16 * 1024 * 1024),
-    )(records, dead_flags.reshape(1, rows))
+    )(records, live)
 
 
 def dft4(a, b, c, d):

time: 47.1 us -> 46.7 us (level)
  local copies, waits for them, and re-layouts: 3.08 us -> 2.41 us
  other arithmetic: 0.07 us -> 0.72 us
    reshape x0 -> x1, other arithmetic: none -> 0.66 us  [deal(): live = (1 - dead_flags).astype(jnp.float32).reshape(1, rows)]
    unnamed x28 -> x26, local copies, waits for them, and re-layouts: 2.33 us -> 1.67 us
where the time goes in v5:
time: 46.7 us; the launch traced here: 46.3 us
  blocking collectives  16.1 us (34%)
  starting transfers between devices  10.7 us (23%)
  Pallas kernels  8.59 us (18%)
  between operations  7.76 us (17%)
  local copies, waits for them, and re-layouts  2.41 us (5%)
  other arithmetic  0.72 us (2%)
    all_to_all x1, blocking collectives, body(): lax.all_to_all(outgoing, 'chan', split_axis=0, concat_axis=0, tiled=True)  16.1 us
    ppermute x4, starting transfers between devices, ahead_on(): lax.ppermute(array, axis, [((i + by) % size, i) for i in range(size)])  10.7 us
    pallas_call x1, Pallas kernels, stack(): pl.pallas_call(stack_kernel, out_shape=jax.ShapeDtypeStruct((2, NOFF, 2 *...  8.04 us
    unnamed x26, local copies, waits for them, and re-layouts  1.67 us
  transfers between devices with their start and end apart: 4, of which 0 were waited for; matrix products, arithmetic and copies ran while one was open for 2% of the time, Pallas kernels for 0%

profile of v5, /device:TPU:1, one launch (start us, length us, event | category | flops | bytes accessed | tf_op | source)
XLA Modules:
  0.0 46.3 jit_solution(10307070964194810337)
XLA Ops:
  0.0 0.7 %convert_bitcast_fusion.live_ref = f32[1,32]{1,0:T(1,128)S(1)} fusion(s32[32]{0:T(128)} %param.13), kind=kLoop, calls=%fused_computation.10 | loop fusion | flops 64 | bytes 256 | tf_op jit(solution)/shard_map/reshape | solution.py:125
  0.7 0.0 copy-start.6
  0.7 0.9 %copy-done.6 = bf16[32,2048]{1,0:T(8,128)(2,1)S(1)} copy-done((bf16[32,2048]{1,0:T(8,128)(2,1)S(1)}, bf16[32,2048]{1,0:T(8,128)(2,1)}, u32[]{:S(2)}) %copy-start.6) | copy-done | bytes 131096
  1.6 0.6 %shard_map.118 = bf16[32,16,128]{2,1,0:T(8,128)(2,1)S(1)} custom-call(bf16[32,2048]{1,0:T(8,128)(2,1)S(1)} %copy-done.6, f32[1,32]{1,0:T(1,128)S(1)} %convert_bitcast_fusion.live_ref), custom_call_target="tpu_custom_call" | custom-call | tf_op jit(solution)/shard_map/pallas_call | solution.py:127
  2.1 6.9 %collective-permute-start = (bf16[32,16,128]{2,1,0:T(8,128)(2,1)S(1)}, bf16[32,16,128]{2,1,0:T(8,128)(2,1)S(1)}, u32[]{:S(2)}, u32[]{:S(2)}) collective-permute-start(bf16[32,16,128]{2,1,0:T(8,128)(2,1)S(1)} %shard_map.118), channel_id=1, source_target_pairs={{16,0},{32,16},{48,32},{64,48},{80,64},{96,80},{112,96},{0,112},{1... | collective-permute-start | bytes 393224 | tf_op jit(solution)/shard_map/ppermute | solution.py:402
  9.1 0.3 collective-permute-start.1
  9.4 0.0 collective-permute-start.2
  9.4 3.4 %collective-permute-start.3 = (bf16[32,16,128]{2,1,0:T(8,128)(2,1)S(1)}, bf16[32,16,128]{2,1,0:T(8,128)(2,1)S(1)}, u32[]{:S(2)}, u32[]{:S(2)}) collective-permute-start(bf16[32,16,128]{2,1,0:T(8,128)(2,1)S(1)} %shard_map.118), channel_id=1, source_target_pairs={{64,0},{80,16},{96,32},{112,48},{0,64},{16,80},{32,96},{48,112},{6... | collective-permute-start | bytes 393224 | tf_op jit(solution)/shard_map/ppermute | solution.py:402
  12.8 0.0 copy-start.10
  12.8 0.6 %copy-done.10 = s32[4]{0:T(128)S(1)} copy-done((s32[4]{0:T(128)S(1)}, s32[4]{0:T(128)}, u32[]{:S(2)}) %copy-start.10) | copy-done | bytes 40
  13.4 0.7 %fusion = (s32[1]{0:T(128)}, s32[1]{0:T(128)}, s32[1]{0:T(128)}, s32[1]{0:T(128)}) fusion(s32[4]{0:T(128)S(1)} %copy-done.10), kind=kLoop, calls=%fused_computation.11 | loop fusion | bytes 32 | tf_op jit(solution)/shard_map/slice | solution.py:413
  21.7 0.0 collective-permute-done
  21.7 0.0 collective-permute-done.1
  21.7 0.0 collective-permute-done.2
  21.8 0.0 collective-permute-done.3
  21.9 0.0 copy-start
  21.9 0.1 pad_maximum_fusion
  22.0 0.0 copy-start.1
  22.0 0.0 copy-start.2
  22.0 0.0 copy-start.3
  22.0 0.0 copy-start.4
  22.0 0.0 copy-start.5
  22.0 0.0 copy-start.7
  22.0 0.0 copy-start.8
  22.0 0.0 copy-start.9
  22.1 16.1 %all_to_all.5.parts_ref = bf16[16,8,16,128]{3,2,1,0:T(8,128)(2,1)S(1)} all-to-all(bf16[16,8,16,128]{3,2,1,0:T(8,128)(2,1)S(1)} %pad_maximum_fusion), channel_id=1, replica_groups=mesh['loop'=8,'chan'=16] {'chan'}, dimensions={0} | all-to-all | bytes 1048576 | tf_op jit(solution)/shard_map/all_to_all | solution.py:419
  38.2 0.0 copy-done
  38.2 0.0 copy-done.1
  38.2 0.0 copy-done.2
  38.2 0.0 copy-done.3
  38.2 0.0 copy-done.4
  38.2 0.0 copy-done.5
  38.2 0.0 copy-done.7
  38.2 0.0 copy-done.8
  38.2 0.0 copy-done.9
  38.2 8.0 %shard_map.119 = f32[2,4,4096]{2,1,0:T(4,128)} custom-call(s32[32]{0:T(128)S(1)} %copy-done.9, bf16[16,8,16,128]{3,2,1,0:T(8,128)(2,1)S(1)} %all_to_all.5.parts_ref, bf16[256,256]{1,0:T(8,128)(2,1)S(1)} %copy-done.2, bf16[256,256]{1,0:T(8,128)(2,1)S(1)} %copy-done.3, bf16[256,256]{1,0:T(8,128)(2,1)S(1)} %copy-done.4, f32[32,8,128]{2,1,0:T(8,128)S(1)} %copy-done.5, ...), custom_call_target="tpu_custom_call" | custom-call | tf_op jit(solution)/shard_map/pallas_call | solution.py:376
  (6 shorter events, 0.1 us)
Async XLA Ops:
  0.7 0.9 %copy-start.6 = (bf16[32,2048]{1,0:T(8,128)(2,1)S(1)}, bf16[32,2048]{1,0:T(8,128)(2,1)}, u32[]{:S(2)}) copy-start(bf16[32,2048]{1,0:T(8,128)(2,1)} %records_ref.1) | copy-start | bytes 393220
  2.1 19.5 %collective-permute-start = (bf16[32,16,128]{2,1,0:T(8,128)(2,1)S(1)}, bf16[32,16,128]{2,1,0:T(8,128)(2,1)S(1)}, u32[]{:S(2)}, u32[]{:S(2)}) collective-permute-start(bf16[32,16,128]{2,1,0:T(8,128)(2,1)S(1)} %shard_map.118), channel_id=1, source_target_pairs={{16,0},{32,16},{48,32},{64,48},{80,64},{96,80},{112,96},{0,112},{1... | collective-permute-start | bytes 393224 | tf_op jit(solution)/shard_map/ppermute | solution.py:402
  9.1 12.6 %collective-permute-start.1 = (bf16[32,16,128]{2,1,0:T(8,128)(2,1)S(1)}, bf16[32,16,128]{2,1,0:T(8,128)(2,1)S(1)}, u32[]{:S(2)}, u32[]{:S(2)}) collective-permute-start(bf16[32,16,128]{2,1,0:T(8,128)(2,1)S(1)} %shard_map.118), channel_id=1, source_target_pairs={{32,0},{48,16},{64,32},{80,48},{96,64},{112,80},{0,96},{16,112},{3... | collective-permute-start | bytes 393224 | tf_op jit(solution)/shard_map/ppermute | solution.py:402
  9.4 12.3 %collective-permute-start.2 = (bf16[32,16,128]{2,1,0:T(8,128)(2,1)S(1)}, bf16[32,16,128]{2,1,0:T(8,128)(2,1)S(1)}, u32[]{:S(2)}, u32[]{:S(2)}) collective-permute-start(bf16[32,16,128]{2,1,0:T(8,128)(2,1)S(1)} %shard_map.118), channel_id=1, source_target_pairs={{48,0},{64,16},{80,32},{96,48},{112,64},{0,80},{16,96},{32,112},{4... | collective-permute-start | bytes 393224 | tf_op jit(solution)/shard_map/ppermute | solution.py:402
  9.4 12.4 %collective-permute-start.3 = (bf16[32,16,128]{2,1,0:T(8,128)(2,1)S(1)}, bf16[32,16,128]{2,1,0:T(8,128)(2,1)S(1)}, u32[]{:S(2)}, u32[]{:S(2)}) collective-permute-start(bf16[32,16,128]{2,1,0:T(8,128)(2,1)S(1)} %shard_map.118), channel_id=1, source_target_pairs={{64,0},{80,16},{96,32},{112,48},{0,64},{16,80},{32,96},{48,112},{6... | collective-permute-start | bytes 393224 | tf_op jit(solution)/shard_map/ppermute | solution.py:402
  12.8 0.7 %copy-start.10 = (s32[4]{0:T(128)S(1)}, s32[4]{0:T(128)}, u32[]{:S(2)}) copy-start(s32[4]{0:T(128)} %param.15) | copy-start | bytes 52
  21.9 16.3 %copy-start = (bf16[16,256,128]{2,1,0:T(8,128)(2,1)S(1)}, bf16[16,256,128]{2,1,0:T(8,128)(2,1)}, u32[]{:S(2)}) copy-start(bf16[16,256,128]{2,1,0:T(8,128)(2,1)} %constant.26.clone.middle_ref) | copy-start | bytes 3145732
  22.0 16.2 %copy-start.1 = (bf16[512,256]{1,0:T(8,128)(2,1)S(1)}, bf16[512,256]{1,0:T(8,128)(2,1)}, u32[]{:S(2)}) copy-start(bf16[512,256]{1,0:T(8,128)(2,1)} %constant.27.clone.box_ref) | copy-start | bytes 786436
  22.0 16.2 %copy-start.2 = (bf16[256,256]{1,0:T(8,128)(2,1)S(1)}, bf16[256,256]{1,0:T(8,128)(2,1)}, u32[]{:S(2)}) copy-start(bf16[256,256]{1,0:T(8,128)(2,1)} %constant.22.clone.shift_ref) | copy-start | bytes 393220
  22.0 16.2 %copy-start.3 = (bf16[256,256]{1,0:T(8,128)(2,1)S(1)}, bf16[256,256]{1,0:T(8,128)(2,1)}, u32[]{:S(2)}) copy-start(bf16[256,256]{1,0:T(8,128)(2,1)} %constant.23.clone.high_ref) | copy-start | bytes 393220
  22.0 16.2 %copy-start.4 = (bf16[256,256]{1,0:T(8,128)(2,1)S(1)}, bf16[256,256]{1,0:T(8,128)(2,1)}, u32[]{:S(2)}) copy-start(bf16[256,256]{1,0:T(8,128)(2,1)} %constant.24.clone.low_ref) | copy-start | bytes 393220
  22.0 16.2 %copy-start.5 = (f32[32,8,128]{2,1,0:T(8,128)S(1)}, f32[32,8,128]{2,1,0:T(8,128)}, u32[]{:S(2)}) copy-start(f32[32,8,128]{2,1,0:T(8,128)} %constant.25.clone.twiddle_ref) | copy-start | bytes 393220
  22.0 16.2 %copy-start.7 = (f32[16,8,128]{2,1,0:T(8,128)S(1)}, f32[16,8,128]{2,1,0:T(8,128)}, u32[]{:S(2)}) copy-start(f32[16,8,128]{2,1,0:T(8,128)} %constant.28.clone.inverse_ref) | copy-start | bytes 196612
  22.0 16.2 %copy-start.8 = (f32[128,128]{1,0:T(8,128)S(1)}, f32[128,128]{1,0:T(8,128)}, u32[]{:S(2)}) copy-start(f32[128,128]{1,0:T(8,128)} %constant.29.clone.flip_ref) | copy-start | bytes 196612
  22.0 16.2 %copy-start.9 = (s32[32]{0:T(128)S(1)}, s32[32]{0:T(128)}, u32[]{:S(2)}) copy-start(s32[32]{0:T(128)} %starts_ref.1) | copy-start | bytes 388

commit v6 on v5

--- a/solution.py
+++ b/solution.py
@@ -397,6 +397,32 @@
     )(starts, parts, *[jnp.asarray(table) for table in tables()])
 
 
+def gather_kernel(offsets_ref, *refs):
+    blocks, out_ref, nearby = refs[:-2], refs[-2], refs[-1]
+    rows = blocks[0].shape[0]
+    for index, block in enumerate(blocks):
+        nearby[pl.ds(index * rows, rows)] = block[...]
+    pair = ROWS // NOFF
+    for o in range(NOFF):
+        offset = offsets_ref[o]
+        for member in range(out_ref.shape[0]):
+            part = nearby[pl.ds(offset + pair * member, pair)]
+            out_ref[member, pl.ds(pair * o, pair)] = part
+
+
+def gather(blocks, offsets, members):
+    rows = blocks[0].shape[0]
+    vmem = pl.BlockSpec(memory_space=pltpu.VMEM)
+    return pl.pallas_call(
+        gather_kernel,
+        out_shape=jax.ShapeDtypeStruct((members, ROWS, PHASES, LANES), jnp.bfloat16),
+        in_specs=[pl.BlockSpec(memory_space=pltpu.SMEM)] + [vmem] * len(blocks),
+        out_specs=vmem,
+        scratch_shapes=[pltpu.VMEM((len(blocks) * rows, PHASES, LANES), jnp.bfloat16)],
+        compiler_params=pltpu.CompilerParams(vmem_limit_bytes=16 * 1024 * 1024),
+    )(offsets, *blocks)
+
+
 def ahead_on(array, axis, by):
     size = lax.axis_size(axis)
     return lax.ppermute(array, axis, [((i + by) % size, i) for i in range(size)])
@@ -407,15 +433,7 @@
     dealt = deal(records, dead_flags)
     reach = lax.axis_size("loop") // 2
     blocks = [dealt] + [ahead_on(dealt, "loop", by) for by in range(1, reach + 1)]
-    nearby = jnp.concatenate(blocks, axis=0)
-    members = lax.axis_size("chan")
-    picked = [
-        lax.dynamic_slice_in_dim(nearby, offsets[o], rows, 0).reshape(
-            members, rows // members, PHASES, LANES
-        )
-        for o in range(NOFF)
-    ]
-    outgoing = jnp.concatenate(picked, axis=1)
+    outgoing = gather(blocks, offsets, lax.axis_size("chan"))
     parts = lax.all_to_all(outgoing, "chan", split_axis=0, concat_axis=0, tiled=True)
     return stack(parts, starts)
 

time: 46.7 us -> 43.8 us (0.938)
  the two profiles are of different devices: /device:TPU:1 before, /device:TPU:24 now
where the time goes in v6:
time: 43.8 us; the launch traced here: 43.6 us
  blocking collectives  15.7 us (36%)
  waiting for transfers between devices  10.7 us (24%)
  Pallas kernels  9.21 us (21%)
  starting transfers between devices  6.29 us (14%)
  local copies, waits for them, and re-layouts  0.97 us (2%)
  other arithmetic  0.66 us (2%)
    all_to_all x1, blocking collectives, body(): lax.all_to_all(outgoing, 'chan', split_axis=0, concat_axis=0, tiled=True)  15.7 us
    ppermute x4, waiting for transfers between devices, ahead_on(): lax.ppermute(array, axis, [((i + by) % size, i) for i in range(size)])  10.7 us
    pallas_call x1, Pallas kernels, stack(): pl.pallas_call(stack_kernel, out_shape=jax.ShapeDtypeStruct((2, NOFF, 2 *...  8.04 us
    ppermute x4, starting transfers between devices, ahead_on(): lax.ppermute(array, axis, [((i + by) % size, i) for i in range(size)])  6.29 us
    unnamed x22, local copies, waits for them, and re-layouts  0.97 us
  transfers between devices with their start and end apart: 4, of which 2 were waited for; matrix products, arithmetic and copies ran while one was open for 0% of the time, Pallas kernels for 0%

profile of v6, /device:TPU:24, one launch (start us, length us, event | category | flops | bytes accessed | tf_op | source)
XLA Modules:
  0.0 43.6 jit_solution(6125259130781366822)
XLA Ops:
  0.0 0.7 %convert_bitcast_fusion.live_ref = f32[1,32]{1,0:T(1,128)S(1)} fusion(s32[32]{0:T(128)} %param.13), kind=kLoop, calls=%fused_computation | loop fusion | flops 64 | bytes 256 | tf_op jit(solution)/shard_map/reshape | solution.py:125
  0.7 0.0 copy-start.6
  0.7 0.9 %copy-done.6 = bf16[32,2048]{1,0:T(8,128)(2,1)S(1)} copy-done((bf16[32,2048]{1,0:T(8,128)(2,1)S(1)}, bf16[32,2048]{1,0:T(8,128)(2,1)}, u32[]{:S(2)}) %copy-start.6) | copy-done | bytes 131096
  1.6 0.0 copy-start.9
  1.6 0.6 %shard_map.118.refs_0_ = bf16[32,16,128]{2,1,0:T(8,128)(2,1)S(1)} custom-call(bf16[32,2048]{1,0:T(8,128)(2,1)S(1)} %copy-done.6, f32[1,32]{1,0:T(1,128)S(1)} %convert_bitcast_fusion.live_ref), custom_call_target="tpu_custom_call" | custom-call | tf_op jit(solution)/shard_map/pallas_call | solution.py:127
  2.1 0.0 copy-start
  2.1 4.0 %collective-permute-start.3 = (bf16[32,16,128]{2,1,0:T(8,128)(2,1)S(1)}, bf16[32,16,128]{2,1,0:T(8,128)(2,1)S(1)}, u32[]{:S(2)}, u32[]{:S(2)}) collective-permute-start(bf16[32,16,128]{2,1,0:T(8,128)(2,1)S(1)} %shard_map.118.refs_0_), channel_id=1, source_target_pairs={{64,0},{80,16},{96,32},{112,48},{0,64},{16,80},{32,96},{48,112},{6... | collective-permute-start | bytes 393224 | tf_op jit(solution)/shard_map/ppermute | solution.py:428
  6.1 0.2 collective-permute-start.2
  6.3 2.1 %collective-permute-start.1 = (bf16[32,16,128]{2,1,0:T(8,128)(2,1)S(1)}, bf16[32,16,128]{2,1,0:T(8,128)(2,1)S(1)}, u32[]{:S(2)}, u32[]{:S(2)}) collective-permute-start(bf16[32,16,128]{2,1,0:T(8,128)(2,1)S(1)} %shard_map.118.refs_0_), channel_id=1, source_target_pairs={{32,0},{48,16},{64,32},{80,48},{96,64},{112,80},{0,96},{16,112},{3... | collective-permute-start | bytes 393224 | tf_op jit(solution)/shard_map/ppermute | solution.py:428
  8.4 0.0 collective-permute-start
  8.4 8.8 %collective-permute-done.3.refs_4_ = bf16[32,16,128]{2,1,0:T(8,128)(2,1)S(1)} collective-permute-done((bf16[32,16,128]{2,1,0:T(8,128)(2,1)S(1)}, bf16[32,16,128]{2,1,0:T(8,128)(2,1)S(1)}, u32[]{:S(2)}, u32[]{:S(2)}) %collective-permute-start.3) | collective-permute-done | bytes 131104 | tf_op jit(solution)/shard_map/ppermute | solution.py:428
  17.3 0.0 collective-permute-done.2.refs_3_
  17.3 0.0 collective-permute-done.1.refs_2_
  17.3 1.9 %collective-permute-done.refs_1_ = bf16[32,16,128]{2,1,0:T(8,128)(2,1)S(1)} collective-permute-done((bf16[32,16,128]{2,1,0:T(8,128)(2,1)S(1)}, bf16[32,16,128]{2,1,0:T(8,128)(2,1)S(1)}, u32[]{:S(2)}, u32[]{:S(2)}) %collective-permute-start) | collective-permute-done | bytes 131104 | tf_op jit(solution)/shard_map/ppermute | solution.py:428
  19.1 0.0 copy-done.9
  19.2 0.6 %shard_map.119 = bf16[16,8,16,128]{3,2,1,0:T(8,128)(2,1)S(1)} custom-call(s32[4]{0:T(128)S(1)} %copy-done.9, bf16[32,16,128]{2,1,0:T(8,128)(2,1)S(1)} %shard_map.118.refs_0_, bf16[32,16,128]{2,1,0:T(8,128)(2,1)S(1)} %collective-permute-done.refs_1_, bf16[32,16,128]{2,1,0:T(8,128)(2,1)S(1)} %collective-permute-done.1.refs_2_, ...), custom_call_target="tpu_custom_call" | custom-call | tf_op jit(solution)/shard_map/pallas_call | solution.py:416
  19.8 0.0 copy-start.1
  19.8 0.0 copy-start.2
  19.8 0.0 copy-start.3
  19.8 0.0 copy-start.4
  19.8 0.0 copy-start.5
  19.8 0.0 copy-start.7
  19.9 0.0 copy-start.8
  19.9 0.0 copy-start.10
  19.9 15.7 %all_to_all.5.parts_ref = bf16[16,8,16,128]{3,2,1,0:T(8,128)(2,1)S(1)} all-to-all(bf16[16,8,16,128]{3,2,1,0:T(8,128)(2,1)S(1)} %shard_map.119), channel_id=1, replica_groups=mesh['loop'=8,'chan'=16] {'chan'}, dimensions={0} | all-to-all | bytes 1048576 | tf_op jit(solution)/shard_map/all_to_all | solution.py:437
  35.5 0.0 copy-done
  35.5 0.0 copy-done.1
  35.5 0.0 copy-done.2
  35.5 0.0 copy-done.3
  35.5 0.0 copy-done.4
  35.6 0.0 copy-done.5
  35.6 0.0 copy-done.7
  35.6 0.0 copy-done.8
  35.6 0.0 copy-done.10
  35.6 8.0 %shard_map.120 = f32[2,4,4096]{2,1,0:T(4,128)} custom-call(s32[32]{0:T(128)S(1)} %copy-done.10, bf16[16,8,16,128]{3,2,1,0:T(8,128)(2,1)S(1)} %all_to_all.5.parts_ref, bf16[256,256]{1,0:T(8,128)(2,1)S(1)} %copy-done.5, bf16[256,256]{1,0:T(8,128)(2,1)S(1)} %copy-done.4, bf16[256,256]{1,0:T(8,128)(2,1)S(1)} %copy-done.3, f32[32,8,128]{2,1,0:T(8,128)S(1)} %copy-done.2, ...), custom_call_target="tpu_custom_call" | custom-call | tf_op jit(solution)/shard_map/pallas_call | solution.py:376
Async XLA Ops:
  0.7 0.9 %copy-start.6 = (bf16[32,2048]{1,0:T(8,128)(2,1)S(1)}, bf16[32,2048]{1,0:T(8,128)(2,1)}, u32[]{:S(2)}) copy-start(bf16[32,2048]{1,0:T(8,128)(2,1)} %records_ref.1) | copy-start | bytes 393220
  1.6 17.6 %copy-start.9 = (s32[4]{0:T(128)S(1)}, s32[4]{0:T(128)}, u32[]{:S(2)}) copy-start(s32[4]{0:T(128)} %offsets_ref.1) | copy-start | bytes 52
  2.1 33.4 %copy-start = (bf16[16,256,128]{2,1,0:T(8,128)(2,1)S(1)}, bf16[16,256,128]{2,1,0:T(8,128)(2,1)}, u32[]{:S(2)}) copy-start(bf16[16,256,128]{2,1,0:T(8,128)(2,1)} %constant.22.clone.middle_ref) | copy-start | bytes 3145732
  2.1 15.1 %collective-permute-start.3 = (bf16[32,16,128]{2,1,0:T(8,128)(2,1)S(1)}, bf16[32,16,128]{2,1,0:T(8,128)(2,1)S(1)}, u32[]{:S(2)}, u32[]{:S(2)}) collective-permute-start(bf16[32,16,128]{2,1,0:T(8,128)(2,1)S(1)} %shard_map.118.refs_0_), channel_id=1, source_target_pairs={{64,0},{80,16},{96,32},{112,48},{0,64},{16,80},{32,96},{48,112},{6... | collective-permute-start | bytes 393224 | tf_op jit(solution)/shard_map/ppermute | solution.py:428
  6.1 11.2 %collective-permute-start.2 = (bf16[32,16,128]{2,1,0:T(8,128)(2,1)S(1)}, bf16[32,16,128]{2,1,0:T(8,128)(2,1)S(1)}, u32[]{:S(2)}, u32[]{:S(2)}) collective-permute-start(bf16[32,16,128]{2,1,0:T(8,128)(2,1)S(1)} %shard_map.118.refs_0_), channel_id=1, source_target_pairs={{48,0},{64,16},{80,32},{96,48},{112,64},{0,80},{16,96},{32,112},{4... | collective-permute-start | bytes 393224 | tf_op jit(solution)/shard_map/ppermute | solution.py:428
  6.3 11.0 %collective-permute-start.1 = (bf16[32,16,128]{2,1,0:T(8,128)(2,1)S(1)}, bf16[32,16,128]{2,1,0:T(8,128)(2,1)S(1)}, u32[]{:S(2)}, u32[]{:S(2)}) collective-permute-start(bf16[32,16,128]{2,1,0:T(8,128)(2,1)S(1)} %shard_map.118.refs_0_), channel_id=1, source_target_pairs={{32,0},{48,16},{64,32},{80,48},{96,64},{112,80},{0,96},{16,112},{3... | collective-permute-start | bytes 393224 | tf_op jit(solution)/shard_map/ppermute | solution.py:428
  8.4 10.7 %collective-permute-start = (bf16[32,16,128]{2,1,0:T(8,128)(2,1)S(1)}, bf16[32,16,128]{2,1,0:T(8,128)(2,1)S(1)}, u32[]{:S(2)}, u32[]{:S(2)}) collective-permute-start(bf16[32,16,128]{2,1,0:T(8,128)(2,1)S(1)} %shard_map.118.refs_0_), channel_id=1, source_target_pairs={{16,0},{32,16},{48,32},{64,48},{80,64},{96,80},{112,96},{0,112},{1... | collective-permute-start | bytes 393224 | tf_op jit(solution)/shard_map/ppermute | solution.py:428
  19.8 15.8 %copy-start.1 = (bf16[512,256]{1,0:T(8,128)(2,1)S(1)}, bf16[512,256]{1,0:T(8,128)(2,1)}, u32[]{:S(2)}) copy-start(bf16[512,256]{1,0:T(8,128)(2,1)} %constant.23.clone.box_ref) | copy-start | bytes 786436
  19.8 15.7 %copy-start.2 = (f32[32,8,128]{2,1,0:T(8,128)S(1)}, f32[32,8,128]{2,1,0:T(8,128)}, u32[]{:S(2)}) copy-start(f32[32,8,128]{2,1,0:T(8,128)} %constant.21.clone.twiddle_ref) | copy-start | bytes 393220
  19.8 15.7 %copy-start.3 = (bf16[256,256]{1,0:T(8,128)(2,1)S(1)}, bf16[256,256]{1,0:T(8,128)(2,1)}, u32[]{:S(2)}) copy-start(bf16[256,256]{1,0:T(8,128)(2,1)} %constant.20.clone.low_ref) | copy-start | bytes 393220
  19.8 15.7 %copy-start.4 = (bf16[256,256]{1,0:T(8,128)(2,1)S(1)}, bf16[256,256]{1,0:T(8,128)(2,1)}, u32[]{:S(2)}) copy-start(bf16[256,256]{1,0:T(8,128)(2,1)} %constant.19.clone.high_ref) | copy-start | bytes 393220
  19.8 15.7 %copy-start.5 = (bf16[256,256]{1,0:T(8,128)(2,1)S(1)}, bf16[256,256]{1,0:T(8,128)(2,1)}, u32[]{:S(2)}) copy-start(bf16[256,256]{1,0:T(8,128)(2,1)} %constant.18.clone.shift_ref) | copy-start | bytes 393220
  19.8 15.7 %copy-start.7 = (f32[128,128]{1,0:T(8,128)S(1)}, f32[128,128]{1,0:T(8,128)}, u32[]{:S(2)}) copy-start(f32[128,128]{1,0:T(8,128)} %constant.25.clone.flip_ref) | copy-start | bytes 196612
  19.9 15.7 %copy-start.8 = (f32[16,8,128]{2,1,0:T(8,128)S(1)}, f32[16,8,128]{2,1,0:T(8,128)}, u32[]{:S(2)}) copy-start(f32[16,8,128]{2,1,0:T(8,128)} %constant.24.clone.inverse_ref) | copy-start | bytes 196612
  19.9 15.7 %copy-start.10 = (s32[32]{0:T(128)S(1)}, s32[32]{0:T(128)}, u32[]{:S(2)}) copy-start(s32[32]{0:T(128)} %starts_ref.1) | copy-start | bytes 388

commit v7 on v6

--- a/solution.py
+++ b/solution.py
@@ -397,10 +397,13 @@
     )(starts, parts, *[jnp.asarray(table) for table in tables()])
 
 
+ORDER = (0, 1, 2, 4, 3)
+
+
 def gather_kernel(offsets_ref, *refs):
     blocks, out_ref, nearby = refs[:-2], refs[-2], refs[-1]
     rows = blocks[0].shape[0]
-    for index, block in enumerate(blocks):
+    for index, block in zip(ORDER, blocks):
         nearby[pl.ds(index * rows, rows)] = block[...]
     pair = ROWS // NOFF
     for o in range(NOFF):
@@ -420,7 +423,7 @@
         out_specs=vmem,
         scratch_shapes=[pltpu.VMEM((len(blocks) * rows, PHASES, LANES), jnp.bfloat16)],
         compiler_params=pltpu.CompilerParams(vmem_limit_bytes=16 * 1024 * 1024),
-    )(offsets, *blocks)
+    )(offsets, *[blocks[index] for index in ORDER])
 
 
 def ahead_on(array, axis, by):

time: 43.8 us -> 43 us (0.982)
  the two profiles are of different devices: /device:TPU:24 before, /device:TPU:1 now
where the time goes in v7:
time: 43 us; the launch traced here: 42.6 us
  blocking collectives  16.7 us (39%)
  starting transfers between devices  11.9 us (28%)
  Pallas kernels  9.2 us (21%)
  waiting for transfers between devices  3.04 us (7%)
  local copies, waits for them, and re-layouts  0.97 us (2%)
  other arithmetic  0.66 us (2%)
    all_to_all x1, blocking collectives, body(): lax.all_to_all(outgoing, 'chan', split_axis=0, concat_axis=0, tiled=True)  16.7 us
    ppermute x4, starting transfers between devices, ahead_on(): lax.ppermute(array, axis, [((i + by) % size, i) for i in range(size)])  11.9 us
    pallas_call x1, Pallas kernels, stack(): pl.pallas_call(stack_kernel, out_shape=jax.ShapeDtypeStruct((2, NOFF, 2 *...  8.04 us
    ppermute x4, waiting for transfers between devices, ahead_on(): lax.ppermute(array, axis, [((i + by) % size, i) for i in range(size)])  3.04 us
    unnamed x22, local copies, waits for them, and re-layouts  0.97 us
  transfers between devices with their start and end apart: 4, of which 2 were waited for; matrix products, arithmetic and copies ran while one was open for 0% of the time, Pallas kernels for 0%

profile of v7, /device:TPU:1, one launch (start us, length us, event | category | flops | bytes accessed | tf_op | source)
XLA Modules:
  0.0 42.6 jit_solution(5011769426586464943)
XLA Ops:
  0.0 0.7 %convert_bitcast_fusion.live_ref = f32[1,32]{1,0:T(1,128)S(1)} fusion(s32[32]{0:T(128)} %param.13), kind=kLoop, calls=%fused_computation | loop fusion | flops 64 | bytes 256 | tf_op jit(solution)/shard_map/reshape | solution.py:125
  0.7 0.0 copy-start.6
  0.7 0.9 %copy-done.6 = bf16[32,2048]{1,0:T(8,128)(2,1)S(1)} copy-done((bf16[32,2048]{1,0:T(8,128)(2,1)S(1)}, bf16[32,2048]{1,0:T(8,128)(2,1)}, u32[]{:S(2)}) %copy-start.6) | copy-done | bytes 131096
  1.6 0.0 copy-start.9
  1.6 0.6 %shard_map.118.refs_0_ = bf16[32,16,128]{2,1,0:T(8,128)(2,1)S(1)} custom-call(bf16[32,2048]{1,0:T(8,128)(2,1)S(1)} %copy-done.6, f32[1,32]{1,0:T(1,128)S(1)} %convert_bitcast_fusion.live_ref), custom_call_target="tpu_custom_call" | custom-call | tf_op jit(solution)/shard_map/pallas_call | solution.py:127
  2.1 0.0 copy-start
  2.1 5.5 %collective-permute-start.3 = (bf16[32,16,128]{2,1,0:T(8,128)(2,1)S(1)}, bf16[32,16,128]{2,1,0:T(8,128)(2,1)S(1)}, u32[]{:S(2)}, u32[]{:S(2)}) collective-permute-start(bf16[32,16,128]{2,1,0:T(8,128)(2,1)S(1)} %shard_map.118.refs_0_), channel_id=1, source_target_pairs={{48,0},{64,16},{80,32},{96,48},{112,64},{0,80},{16,96},{32,112},{4... | collective-permute-start | bytes 393224 | tf_op jit(solution)/shard_map/ppermute | solution.py:431
  7.6 0.0 collective-permute-start.2
  7.6 5.3 %collective-permute-start.1 = (bf16[32,16,128]{2,1,0:T(8,128)(2,1)S(1)}, bf16[32,16,128]{2,1,0:T(8,128)(2,1)S(1)}, u32[]{:S(2)}, u32[]{:S(2)}) collective-permute-start(bf16[32,16,128]{2,1,0:T(8,128)(2,1)S(1)} %shard_map.118.refs_0_), channel_id=1, source_target_pairs={{32,0},{48,16},{64,32},{80,48},{96,64},{112,80},{0,96},{16,112},{3... | collective-permute-start | bytes 393224 | tf_op jit(solution)/shard_map/ppermute | solution.py:431
  12.9 1.1 %collective-permute-start = (bf16[32,16,128]{2,1,0:T(8,128)(2,1)S(1)}, bf16[32,16,128]{2,1,0:T(8,128)(2,1)S(1)}, u32[]{:S(2)}, u32[]{:S(2)}) collective-permute-start(bf16[32,16,128]{2,1,0:T(8,128)(2,1)S(1)} %shard_map.118.refs_0_), channel_id=1, source_target_pairs={{16,0},{32,16},{48,32},{64,48},{80,64},{96,80},{112,96},{0,112},{1... | collective-permute-start | bytes 393224 | tf_op jit(solution)/shard_map/ppermute | solution.py:431
  14.0 0.0 collective-permute-done.3.refs_4_
  14.0 0.0 collective-permute-done.2.refs_3_
  14.0 2.0 %collective-permute-done.1.refs_2_ = bf16[32,16,128]{2,1,0:T(8,128)(2,1)S(1)} collective-permute-done((bf16[32,16,128]{2,1,0:T(8,128)(2,1)S(1)}, bf16[32,16,128]{2,1,0:T(8,128)(2,1)S(1)}, u32[]{:S(2)}, u32[]{:S(2)}) %collective-permute-start.1) | collective-permute-done | bytes 131104 | tf_op jit(solution)/shard_map/ppermute | solution.py:431
  16.1 1.0 %collective-permute-done.refs_1_ = bf16[32,16,128]{2,1,0:T(8,128)(2,1)S(1)} collective-permute-done((bf16[32,16,128]{2,1,0:T(8,128)(2,1)S(1)}, bf16[32,16,128]{2,1,0:T(8,128)(2,1)S(1)}, u32[]{:S(2)}, u32[]{:S(2)}) %collective-permute-start) | collective-permute-done | bytes 131104 | tf_op jit(solution)/shard_map/ppermute | solution.py:431
  17.1 0.0 copy-done.9
  17.1 0.6 %shard_map.119 = bf16[16,8,16,128]{3,2,1,0:T(8,128)(2,1)S(1)} custom-call(s32[4]{0:T(128)S(1)} %copy-done.9, bf16[32,16,128]{2,1,0:T(8,128)(2,1)S(1)} %shard_map.118.refs_0_, bf16[32,16,128]{2,1,0:T(8,128)(2,1)S(1)} %collective-permute-done.refs_1_, bf16[32,16,128]{2,1,0:T(8,128)(2,1)S(1)} %collective-permute-done.1.refs_2_, ...), custom_call_target="tpu_custom_call" | custom-call | tf_op jit(solution)/shard_map/pallas_call | solution.py:419
  17.7 0.0 copy-start.1
  17.7 0.0 copy-start.2
  17.7 0.0 copy-start.3
  17.7 0.0 copy-start.4
  17.7 0.0 copy-start.5
  17.8 0.0 copy-start.7
  17.8 0.0 copy-start.8
  17.8 0.0 copy-start.10
  17.8 16.7 %all_to_all.5.parts_ref = bf16[16,8,16,128]{3,2,1,0:T(8,128)(2,1)S(1)} all-to-all(bf16[16,8,16,128]{3,2,1,0:T(8,128)(2,1)S(1)} %shard_map.119), channel_id=1, replica_groups=mesh['loop'=8,'chan'=16] {'chan'}, dimensions={0} | all-to-all | bytes 1048576 | tf_op jit(solution)/shard_map/all_to_all | solution.py:440
  34.5 0.0 copy-done
  34.5 0.0 copy-done.1
  34.5 0.0 copy-done.2
  34.5 0.0 copy-done.3
  34.5 0.0 copy-done.4
  34.5 0.0 copy-done.5
  34.5 0.0 copy-done.7
  34.5 0.0 copy-done.8
  34.5 0.0 copy-done.10
  34.6 8.0 %shard_map.120 = f32[2,4,4096]{2,1,0:T(4,128)} custom-call(s32[32]{0:T(128)S(1)} %copy-done.10, bf16[16,8,16,128]{3,2,1,0:T(8,128)(2,1)S(1)} %all_to_all.5.parts_ref, bf16[256,256]{1,0:T(8,128)(2,1)S(1)} %copy-done.5, bf16[256,256]{1,0:T(8,128)(2,1)S(1)} %copy-done.4, bf16[256,256]{1,0:T(8,128)(2,1)S(1)} %copy-done.3, f32[32,8,128]{2,1,0:T(8,128)S(1)} %copy-done.2, ...), custom_call_target="tpu_custom_call" | custom-call | tf_op jit(solution)/shard_map/pallas_call | solution.py:376
Async XLA Ops:
  0.7 0.9 %copy-start.6 = (bf16[32,2048]{1,0:T(8,128)(2,1)S(1)}, bf16[32,2048]{1,0:T(8,128)(2,1)}, u32[]{:S(2)}) copy-start(bf16[32,2048]{1,0:T(8,128)(2,1)} %records_ref.1) | copy-start | bytes 393220
  1.6 15.5 %copy-start.9 = (s32[4]{0:T(128)S(1)}, s32[4]{0:T(128)}, u32[]{:S(2)}) copy-start(s32[4]{0:T(128)} %offsets_ref.1) | copy-start | bytes 52
  2.1 32.4 %copy-start = (bf16[16,256,128]{2,1,0:T(8,128)(2,1)S(1)}, bf16[16,256,128]{2,1,0:T(8,128)(2,1)}, u32[]{:S(2)}) copy-start(bf16[16,256,128]{2,1,0:T(8,128)(2,1)} %constant.22.clone.middle_ref) | copy-start | bytes 3145732
  2.1 11.9 %collective-permute-start.3 = (bf16[32,16,128]{2,1,0:T(8,128)(2,1)S(1)}, bf16[32,16,128]{2,1,0:T(8,128)(2,1)S(1)}, u32[]{:S(2)}, u32[]{:S(2)}) collective-permute-start(bf16[32,16,128]{2,1,0:T(8,128)(2,1)S(1)} %shard_map.118.refs_0_), channel_id=1, source_target_pairs={{48,0},{64,16},{80,32},{96,48},{112,64},{0,80},{16,96},{32,112},{4... | collective-permute-start | bytes 393224 | tf_op jit(solution)/shard_map/ppermute | solution.py:431
  7.6 6.4 %collective-permute-start.2 = (bf16[32,16,128]{2,1,0:T(8,128)(2,1)S(1)}, bf16[32,16,128]{2,1,0:T(8,128)(2,1)S(1)}, u32[]{:S(2)}, u32[]{:S(2)}) collective-permute-start(bf16[32,16,128]{2,1,0:T(8,128)(2,1)S(1)} %shard_map.118.refs_0_), channel_id=1, source_target_pairs={{64,0},{80,16},{96,32},{112,48},{0,64},{16,80},{32,96},{48,112},{6... | collective-permute-start | bytes 393224 | tf_op jit(solution)/shard_map/ppermute | solution.py:431
  7.6 8.4 %collective-permute-start.1 = (bf16[32,16,128]{2,1,0:T(8,128)(2,1)S(1)}, bf16[32,16,128]{2,1,0:T(8,128)(2,1)S(1)}, u32[]{:S(2)}, u32[]{:S(2)}) collective-permute-start(bf16[32,16,128]{2,1,0:T(8,128)(2,1)S(1)} %shard_map.118.refs_0_), channel_id=1, source_target_pairs={{32,0},{48,16},{64,32},{80,48},{96,64},{112,80},{0,96},{16,112},{3... | collective-permute-start | bytes 393224 | tf_op jit(solution)/shard_map/ppermute | solution.py:431
  12.9 4.1 %collective-permute-start = (bf16[32,16,128]{2,1,0:T(8,128)(2,1)S(1)}, bf16[32,16,128]{2,1,0:T(8,128)(2,1)S(1)}, u32[]{:S(2)}, u32[]{:S(2)}) collective-permute-start(bf16[32,16,128]{2,1,0:T(8,128)(2,1)S(1)} %shard_map.118.refs_0_), channel_id=1, source_target_pairs={{16,0},{32,16},{48,32},{64,48},{80,64},{96,80},{112,96},{0,112},{1... | collective-permute-start | bytes 393224 | tf_op jit(solution)/shard_map/ppermute | solution.py:431
  17.7 16.8 %copy-start.1 = (bf16[512,256]{1,0:T(8,128)(2,1)S(1)}, bf16[512,256]{1,0:T(8,128)(2,1)}, u32[]{:S(2)}) copy-start(bf16[512,256]{1,0:T(8,128)(2,1)} %constant.23.clone.box_ref) | copy-start | bytes 786436
  17.7 16.8 %copy-start.2 = (f32[32,8,128]{2,1,0:T(8,128)S(1)}, f32[32,8,128]{2,1,0:T(8,128)}, u32[]{:S(2)}) copy-start(f32[32,8,128]{2,1,0:T(8,128)} %constant.21.clone.twiddle_ref) | copy-start | bytes 393220
  17.7 16.8 %copy-start.3 = (bf16[256,256]{1,0:T(8,128)(2,1)S(1)}, bf16[256,256]{1,0:T(8,128)(2,1)}, u32[]{:S(2)}) copy-start(bf16[256,256]{1,0:T(8,128)(2,1)} %constant.20.clone.low_ref) | copy-start | bytes 393220
  17.7 16.8 %copy-start.4 = (bf16[256,256]{1,0:T(8,128)(2,1)S(1)}, bf16[256,256]{1,0:T(8,128)(2,1)}, u32[]{:S(2)}) copy-start(bf16[256,256]{1,0:T(8,128)(2,1)} %constant.19.clone.high_ref) | copy-start | bytes 393220
  17.7 16.8 %copy-start.5 = (bf16[256,256]{1,0:T(8,128)(2,1)S(1)}, bf16[256,256]{1,0:T(8,128)(2,1)}, u32[]{:S(2)}) copy-start(bf16[256,256]{1,0:T(8,128)(2,1)} %constant.18.clone.shift_ref) | copy-start | bytes 393220
  17.8 16.8 %copy-start.7 = (f32[128,128]{1,0:T(8,128)S(1)}, f32[128,128]{1,0:T(8,128)}, u32[]{:S(2)}) copy-start(f32[128,128]{1,0:T(8,128)} %constant.25.clone.flip_ref) | copy-start | bytes 196612
  17.8 16.8 %copy-start.8 = (f32[16,8,128]{2,1,0:T(8,128)S(1)}, f32[16,8,128]{2,1,0:T(8,128)}, u32[]{:S(2)}) copy-start(f32[16,8,128]{2,1,0:T(8,128)} %constant.24.clone.inverse_ref) | copy-start | bytes 196612
  17.8 16.8 %copy-start.10 = (s32[32]{0:T(128)S(1)}, s32[32]{0:T(128)}, u32[]{:S(2)}) copy-start(s32[32]{0:T(128)} %starts_ref.1) | copy-start | bytes 388

commit v8 on v7

--- a/solution.py
+++ b/solution.py
@@ -129,7 +129,7 @@
         out_shape=jax.ShapeDtypeStruct((rows, PHASES, LANES), jnp.bfloat16),
         in_specs=[vmem] * 2,
         out_specs=vmem,
-        scratch_shapes=[pltpu.VMEM((rows * PITCH, LANES), jnp.float32)],
+        scratch_shapes=[pltpu.VMEM(((rows + 1) * PITCH - 1, LANES), jnp.float32)],
         compiler_params=pltpu.CompilerParams(vmem_limit_bytes=16 * 1024 * 1024),
     )(records, live)
 
@@ -379,11 +379,11 @@
         in_specs=[pl.BlockSpec(memory_space=pltpu.SMEM)] + [vmem] * 9,
         out_specs=vmem,
         scratch_shapes=[
-            pltpu.VMEM((shards, ROWS * PITCH, LANES), f32),
+            pltpu.VMEM((shards, (ROWS + 1) * PITCH - 1, LANES), f32),
             pltpu.VMEM((shards + 2, PHASES * ROWS, LANES), jnp.bfloat16),
             pltpu.VMEM((shards + 1, PHASES * ROWS, 2 * LANES), f32),
             pltpu.VMEM((PHASES, shards + 2, ROWS, LANES), f32),
-            pltpu.VMEM((2 * PHASES, ROWS * (NWIN + 1), LANES), f32),
+            pltpu.VMEM((2 * PHASES, (ROWS + 1) * (NWIN + 1) - 1, LANES), f32),
             pltpu.VMEM((PHASES, SEGS, 2 * LANES), jnp.bfloat16),
             pltpu.VMEM((PHASES, SEGS, 2 * LANES), f32),
             pltpu.VMEM((SEGS, LANES), f32),
@@ -391,7 +391,7 @@
             pltpu.VMEM((SEGS, (2 * GROUPS + 2) * LANES), jnp.bfloat16),
             pltpu.VMEM((GROUPS, SEGS, 2 * LANES), f32),
             pltpu.VMEM((2 * GROUPS * 8, LANES), f32),
-            pltpu.VMEM((4 * GROUPS, 72, LANES), f32),
+            pltpu.VMEM((4 * GROUPS, 80, LANES), f32),
         ],
         compiler_params=pltpu.CompilerParams(vmem_limit_bytes=40 * 1024 * 1024),
     )(starts, parts, *[jnp.asarray(table) for table in tables()])

time: 43 us -> 43 us (level)
  no operation moved by 1% of the time
where the time goes in v8:
time: 43 us; the launch traced here: 42.6 us
  blocking collectives  16.7 us (39%)
  starting transfers between devices  11.9 us (28%)
  Pallas kernels  9.2 us (21%)
  waiting for transfers between devices  3.04 us (7%)
  local copies, waits for them, and re-layouts  0.97 us (2%)
  other arithmetic  0.66 us (2%)
    all_to_all x1, blocking collectives, body(): lax.all_to_all(outgoing, 'chan', split_axis=0, concat_axis=0, tiled=True)  16.7 us
    ppermute x4, starting transfers between devices, ahead_on(): lax.ppermute(array, axis, [((i + by) % size, i) for i in range(size)])  11.9 us
    pallas_call x1, Pallas kernels, stack(): pl.pallas_call(stack_kernel, out_shape=jax.ShapeDtypeStruct((2, NOFF, 2 *...  8.03 us
    ppermute x4, waiting for transfers between devices, ahead_on(): lax.ppermute(array, axis, [((i + by) % size, i) for i in range(size)])  3.04 us
    unnamed x22, local copies, waits for them, and re-layouts  0.97 us
  transfers between devices with their start and end apart: 4, of which 2 were waited for; matrix products, arithmetic and copies ran while one was open for 0% of the time, Pallas kernels for 0%

profile of v8, /device:TPU:1, one launch (start us, length us, event | category | flops | bytes accessed | tf_op | source)
XLA Modules:
  0.0 42.6 jit_solution(15077082644528919905)
XLA Ops:
  0.0 0.7 %convert_bitcast_fusion.live_ref = f32[1,32]{1,0:T(1,128)S(1)} fusion(s32[32]{0:T(128)} %param.13), kind=kLoop, calls=%fused_computation | loop fusion | flops 64 | bytes 256 | tf_op jit(solution)/shard_map/reshape | solution.py:125
  0.7 0.0 copy-start.6
  0.7 0.9 %copy-done.6 = bf16[32,2048]{1,0:T(8,128)(2,1)S(1)} copy-done((bf16[32,2048]{1,0:T(8,128)(2,1)S(1)}, bf16[32,2048]{1,0:T(8,128)(2,1)}, u32[]{:S(2)}) %copy-start.6) | copy-done | bytes 131096
  1.6 0.0 copy-start.9
  1.6 0.6 %shard_map.118.refs_0_ = bf16[32,16,128]{2,1,0:T(8,128)(2,1)S(1)} custom-call(bf16[32,2048]{1,0:T(8,128)(2,1)S(1)} %copy-done.6, f32[1,32]{1,0:T(1,128)S(1)} %convert_bitcast_fusion.live_ref), custom_call_target="tpu_custom_call" | custom-call | tf_op jit(solution)/shard_map/pallas_call | solution.py:127
  2.1 0.0 copy-start
  2.1 5.5 %collective-permute-start.3 = (bf16[32,16,128]{2,1,0:T(8,128)(2,1)S(1)}, bf16[32,16,128]{2,1,0:T(8,128)(2,1)S(1)}, u32[]{:S(2)}, u32[]{:S(2)}) collective-permute-start(bf16[32,16,128]{2,1,0:T(8,128)(2,1)S(1)} %shard_map.118.refs_0_), channel_id=1, source_target_pairs={{48,0},{64,16},{80,32},{96,48},{112,64},{0,80},{16,96},{32,112},{4... | collective-permute-start | bytes 393224 | tf_op jit(solution)/shard_map/ppermute | solution.py:431
  7.6 0.0 collective-permute-start.2
  7.6 5.3 %collective-permute-start.1 = (bf16[32,16,128]{2,1,0:T(8,128)(2,1)S(1)}, bf16[32,16,128]{2,1,0:T(8,128)(2,1)S(1)}, u32[]{:S(2)}, u32[]{:S(2)}) collective-permute-start(bf16[32,16,128]{2,1,0:T(8,128)(2,1)S(1)} %shard_map.118.refs_0_), channel_id=1, source_target_pairs={{32,0},{48,16},{64,32},{80,48},{96,64},{112,80},{0,96},{16,112},{3... | collective-permute-start | bytes 393224 | tf_op jit(solution)/shard_map/ppermute | solution.py:431
  12.9 1.1 %collective-permute-start = (bf16[32,16,128]{2,1,0:T(8,128)(2,1)S(1)}, bf16[32,16,128]{2,1,0:T(8,128)(2,1)S(1)}, u32[]{:S(2)}, u32[]{:S(2)}) collective-permute-start(bf16[32,16,128]{2,1,0:T(8,128)(2,1)S(1)} %shard_map.118.refs_0_), channel_id=1, source_target_pairs={{16,0},{32,16},{48,32},{64,48},{80,64},{96,80},{112,96},{0,112},{1... | collective-permute-start | bytes 393224 | tf_op jit(solution)/shard_map/ppermute | solution.py:431
  14.0 0.0 collective-permute-done.3.refs_4_
  14.0 0.0 collective-permute-done.2.refs_3_
  14.0 2.0 %collective-permute-done.1.refs_2_ = bf16[32,16,128]{2,1,0:T(8,128)(2,1)S(1)} collective-permute-done((bf16[32,16,128]{2,1,0:T(8,128)(2,1)S(1)}, bf16[32,16,128]{2,1,0:T(8,128)(2,1)S(1)}, u32[]{:S(2)}, u32[]{:S(2)}) %collective-permute-start.1) | collective-permute-done | bytes 131104 | tf_op jit(solution)/shard_map/ppermute | solution.py:431
  16.1 1.0 %collective-permute-done.refs_1_ = bf16[32,16,128]{2,1,0:T(8,128)(2,1)S(1)} collective-permute-done((bf16[32,16,128]{2,1,0:T(8,128)(2,1)S(1)}, bf16[32,16,128]{2,1,0:T(8,128)(2,1)S(1)}, u32[]{:S(2)}, u32[]{:S(2)}) %collective-permute-start) | collective-permute-done | bytes 131104 | tf_op jit(solution)/shard_map/ppermute | solution.py:431
  17.1 0.0 copy-done.9
  17.1 0.6 %shard_map.119 = bf16[16,8,16,128]{3,2,1,0:T(8,128)(2,1)S(1)} custom-call(s32[4]{0:T(128)S(1)} %copy-done.9, bf16[32,16,128]{2,1,0:T(8,128)(2,1)S(1)} %shard_map.118.refs_0_, bf16[32,16,128]{2,1,0:T(8,128)(2,1)S(1)} %collective-permute-done.refs_1_, bf16[32,16,128]{2,1,0:T(8,128)(2,1)S(1)} %collective-permute-done.1.refs_2_, ...), custom_call_target="tpu_custom_call" | custom-call | tf_op jit(solution)/shard_map/pallas_call | solution.py:419
  17.7 0.0 copy-start.1
  17.7 0.0 copy-start.2
  17.7 0.0 copy-start.3
  17.7 0.0 copy-start.4
  17.7 0.0 copy-start.5
  17.8 0.0 copy-start.7
  17.8 0.0 copy-start.8
  17.8 0.0 copy-start.10
  17.8 16.7 %all_to_all.5.parts_ref = bf16[16,8,16,128]{3,2,1,0:T(8,128)(2,1)S(1)} all-to-all(bf16[16,8,16,128]{3,2,1,0:T(8,128)(2,1)S(1)} %shard_map.119), channel_id=1, replica_groups=mesh['loop'=8,'chan'=16] {'chan'}, dimensions={0} | all-to-all | bytes 1048576 | tf_op jit(solution)/shard_map/all_to_all | solution.py:440
  34.5 0.0 copy-done
  34.5 0.0 copy-done.1
  34.5 0.0 copy-done.2
  34.5 0.0 copy-done.3
  34.5 0.0 copy-done.4
  34.5 0.0 copy-done.5
  34.5 0.0 copy-done.7
  34.5 0.0 copy-done.8
  34.5 0.0 copy-done.10
  34.6 8.0 %shard_map.120 = f32[2,4,4096]{2,1,0:T(4,128)} custom-call(s32[32]{0:T(128)S(1)} %copy-done.10, bf16[16,8,16,128]{3,2,1,0:T(8,128)(2,1)S(1)} %all_to_all.5.parts_ref, bf16[256,256]{1,0:T(8,128)(2,1)S(1)} %copy-done.5, bf16[256,256]{1,0:T(8,128)(2,1)S(1)} %copy-done.4, bf16[256,256]{1,0:T(8,128)(2,1)S(1)} %copy-done.3, f32[32,8,128]{2,1,0:T(8,128)S(1)} %copy-done.2, ...), custom_call_target="tpu_custom_call" | custom-call | tf_op jit(solution)/shard_map/pallas_call | solution.py:376
Async XLA Ops:
  0.7 0.9 %copy-start.6 = (bf16[32,2048]{1,0:T(8,128)(2,1)S(1)}, bf16[32,2048]{1,0:T(8,128)(2,1)}, u32[]{:S(2)}) copy-start(bf16[32,2048]{1,0:T(8,128)(2,1)} %records_ref.1) | copy-start | bytes 393220
  1.6 15.5 %copy-start.9 = (s32[4]{0:T(128)S(1)}, s32[4]{0:T(128)}, u32[]{:S(2)}) copy-start(s32[4]{0:T(128)} %offsets_ref.1) | copy-start | bytes 52
  2.1 32.4 %copy-start = (bf16[16,256,128]{2,1,0:T(8,128)(2,1)S(1)}, bf16[16,256,128]{2,1,0:T(8,128)(2,1)}, u32[]{:S(2)}) copy-start(bf16[16,256,128]{2,1,0:T(8,128)(2,1)} %constant.22.clone.middle_ref) | copy-start | bytes 3145732
  2.1 11.9 %collective-permute-start.3 = (bf16[32,16,128]{2,1,0:T(8,128)(2,1)S(1)}, bf16[32,16,128]{2,1,0:T(8,128)(2,1)S(1)}, u32[]{:S(2)}, u32[]{:S(2)}) collective-permute-start(bf16[32,16,128]{2,1,0:T(8,128)(2,1)S(1)} %shard_map.118.refs_0_), channel_id=1, source_target_pairs={{48,0},{64,16},{80,32},{96,48},{112,64},{0,80},{16,96},{32,112},{4... | collective-permute-start | bytes 393224 | tf_op jit(solution)/shard_map/ppermute | solution.py:431
  7.6 6.4 %collective-permute-start.2 = (bf16[32,16,128]{2,1,0:T(8,128)(2,1)S(1)}, bf16[32,16,128]{2,1,0:T(8,128)(2,1)S(1)}, u32[]{:S(2)}, u32[]{:S(2)}) collective-permute-start(bf16[32,16,128]{2,1,0:T(8,128)(2,1)S(1)} %shard_map.118.refs_0_), channel_id=1, source_target_pairs={{64,0},{80,16},{96,32},{112,48},{0,64},{16,80},{32,96},{48,112},{6... | collective-permute-start | bytes 393224 | tf_op jit(solution)/shard_map/ppermute | solution.py:431
  7.6 8.4 %collective-permute-start.1 = (bf16[32,16,128]{2,1,0:T(8,128)(2,1)S(1)}, bf16[32,16,128]{2,1,0:T(8,128)(2,1)S(1)}, u32[]{:S(2)}, u32[]{:S(2)}) collective-permute-start(bf16[32,16,128]{2,1,0:T(8,128)(2,1)S(1)} %shard_map.118.refs_0_), channel_id=1, source_target_pairs={{32,0},{48,16},{64,32},{80,48},{96,64},{112,80},{0,96},{16,112},{3... | collective-permute-start | bytes 393224 | tf_op jit(solution)/shard_map/ppermute | solution.py:431
  12.9 4.1 %collective-permute-start = (bf16[32,16,128]{2,1,0:T(8,128)(2,1)S(1)}, bf16[32,16,128]{2,1,0:T(8,128)(2,1)S(1)}, u32[]{:S(2)}, u32[]{:S(2)}) collective-permute-start(bf16[32,16,128]{2,1,0:T(8,128)(2,1)S(1)} %shard_map.118.refs_0_), channel_id=1, source_target_pairs={{16,0},{32,16},{48,32},{64,48},{80,64},{96,80},{112,96},{0,112},{1... | collective-permute-start | bytes 393224 | tf_op jit(solution)/shard_map/ppermute | solution.py:431
  17.7 16.8 %copy-start.1 = (bf16[512,256]{1,0:T(8,128)(2,1)S(1)}, bf16[512,256]{1,0:T(8,128)(2,1)}, u32[]{:S(2)}) copy-start(bf16[512,256]{1,0:T(8,128)(2,1)} %constant.23.clone.box_ref) | copy-start | bytes 786436
  17.7 16.8 %copy-start.2 = (f32[32,8,128]{2,1,0:T(8,128)S(1)}, f32[32,8,128]{2,1,0:T(8,128)}, u32[]{:S(2)}) copy-start(f32[32,8,128]{2,1,0:T(8,128)} %constant.21.clone.twiddle_ref) | copy-start | bytes 393220
  17.7 16.8 %copy-start.3 = (bf16[256,256]{1,0:T(8,128)(2,1)S(1)}, bf16[256,256]{1,0:T(8,128)(2,1)}, u32[]{:S(2)}) copy-start(bf16[256,256]{1,0:T(8,128)(2,1)} %constant.20.clone.low_ref) | copy-start | bytes 393220
  17.7 16.8 %copy-start.4 = (bf16[256,256]{1,0:T(8,128)(2,1)S(1)}, bf16[256,256]{1,0:T(8,128)(2,1)}, u32[]{:S(2)}) copy-start(bf16[256,256]{1,0:T(8,128)(2,1)} %constant.19.clone.high_ref) | copy-start | bytes 393220
  17.7 16.8 %copy-start.5 = (bf16[256,256]{1,0:T(8,128)(2,1)S(1)}, bf16[256,256]{1,0:T(8,128)(2,1)}, u32[]{:S(2)}) copy-start(bf16[256,256]{1,0:T(8,128)(2,1)} %constant.18.clone.shift_ref) | copy-start | bytes 393220
  17.8 16.8 %copy-start.7 = (f32[128,128]{1,0:T(8,128)S(1)}, f32[128,128]{1,0:T(8,128)}, u32[]{:S(2)}) copy-start(f32[128,128]{1,0:T(8,128)} %constant.25.clone.flip_ref) | copy-start | bytes 196612
  17.8 16.8 %copy-start.8 = (f32[16,8,128]{2,1,0:T(8,128)S(1)}, f32[16,8,128]{2,1,0:T(8,128)}, u32[]{:S(2)}) copy-start(f32[16,8,128]{2,1,0:T(8,128)} %constant.24.clone.inverse_ref) | copy-start | bytes 196612
  17.8 16.8 %copy-start.10 = (s32[32]{0:T(128)S(1)}, s32[32]{0:T(128)}, u32[]{:S(2)}) copy-start(s32[32]{0:T(128)} %starts_ref.1) | copy-start | bytes 388
